TPU v7x, 32 devices: a whole 2x2x4 slice. The times are simulated.
32 devices in a mesh: section: 2 (over core), shard: 4 (over y, x), replica: 4 (over z).
Axes of the slice: x: 2, y: 2, z: 4, core: 2. Of those that a mesh axis runs over, the one named last changes fastest.
Arguments:
- boundary: bfloat16 [2, 4, 48, 14, 14, 512], P('section', None, ('shard', 'replica')), may hold values from -6 to 6
- norm_gains: bfloat16 [2, 2, 512], P('section', None, 'shard'), may hold values from 0.5 to 1.5
- biases: bfloat16 [2, 6, 512], P('section', None, 'shard'), may hold values from -3 to 3
- up_bias: bfloat16 [2, 2048], P('section', 'shard'), may hold values from -3 to 3
- offset_table: bfloat16 [2, 169, 16], P('section', None, 'shard'), may hold values from -4 to 4
- attention_in: bfloat16 [2, 512, 1536], P('section', 'shard'), may hold values from -0.25 to 0.25
- attention_out: bfloat16 [2, 512, 512], P('section', 'shard'), may hold values from -1 to 1
- up_weight: bfloat16 [2, 512, 2048], P('section', 'shard'), may hold values from -0.25 to 0.25
- down_weight: bfloat16 [2, 2048, 512], P('section', 'shard'), may hold values from -0.125 to 0.125
- offset_index: int32 [49, 49], replicated, may hold values from 0 to 168
- regions: int32 [14, 14], replicated, may hold values from 0 to 3
- micro_counts: int32 [4], replicated, may hold values from 1 to 3, as said below
Outputs:
- results: bfloat16 [2, 4, 48, 14, 14, 512], P('section', None, ('shard', 'replica'))
- grad_norm_gains: float32 [2, 2, 512], P('section', None, 'shard')
- grad_biases: float32 [2, 6, 512], P('section', None, 'shard')
- grad_up_bias: float32 [2, 2048], P('section', 'shard')
- grad_offset_table: float32 [2, 169, 16], P('section', None, 'shard')
- grad_attention_in: float32 [2, 512, 1536], P('section', 'shard')
- grad_attention_out: float32 [2, 512, 512], P('section', 'shard')
- grad_up_weight: float32 [2, 512, 2048], P('section', 'shard')
- grad_down_weight: float32 [2, 2048, 512], P('section', 'shard')
Inputs may be any that keep to these rules, and one draw needn't show every extreme that they name: `micro_counts`: in every draw one micro-batch has all 3 slots filled.
All inputs are finite; a program needn't handle non-finite values.
Results may differ from a plain program's by a relative error of at most 0.02.
Values may be sent and summed in bfloat16 or wider, within the bound.
No kernel may reach another device: no remote copies, remote signals or barrier semaphores. Data moves between devices by JAX's collectives and lax.ppermute only.
A program may use at most 384 MiB of HBM per device.

v0:
```python
import functools

import jax
import jax.numpy as jnp
import numpy as np
from jax import lax
from jax.experimental import pallas as pl
from jax.experimental.pallas import tpu as pltpu
from jax.sharding import PartitionSpec as P

WIN = 7
SIDE = 14
SHIFT = 3
LEN = WIN * WIN
WINS = 4
SLOT = 64
ROWS = WINS * SLOT
TOKENS = SIDE * SIDE
FRAME = 208
HEADS = 16
QUAD = 4
GROUPS = HEADS // QUAD
WIDE = QUAD * SLOT
LOG2E = 1.4426950408889634
F32 = jnp.float32
BF16 = jnp.bfloat16


def window_place(shift):
    place = np.zeros((ROWS, FRAME), np.float32)
    for window in range(WINS):
        for token in range(LEN):
            line = ((window // 2) * WIN + token // WIN + shift) % SIDE
            column = ((window % 2) * WIN + token % WIN + shift) % SIDE
            place[window * SLOT + token, line * SIDE + column] = 1.0
    return place


def mm(a, b):
    return jnp.dot(a, b, preferred_element_type=F32)


def mm_nt(a, b):
    return lax.dot_general(a, b, (((1,), (1,)), ((), ())), preferred_element_type=F32)


def mm_tn(a, b):
    return lax.dot_general(a, b, (((0,), (0,)), ((), ())), preferred_element_type=F32)


def standard(v):
    centered = v - jnp.mean(v, -1, keepdims=True)
    spread = jnp.mean(centered * centered, -1, keepdims=True)
    inverse = lax.rsqrt(spread + 1e-05)
    return centered * inverse, inverse


def gelu_pair(h):
    density = jnp.exp(-0.5 * h * h)
    t = 1.0 / (1.0 + (0.3275911 * 0.7071067811865476) * jnp.abs(h))
    poly = t * (
        0.5 * 0.254829592
        + t
        * (
            0.5 * -0.284496736
            + t * (0.5 * 1.421413741 + t * (0.5 * -1.453152027 + t * (0.5 * 1.061405429)))
        )
    )
    tail = poly * density
    cdf = jnp.where(h < 0, tail, 1.0 - tail)
    return h * cdf, cdf + h * (density * 0.3989422804014327)


def head_mask(shape):
    rows = lax.broadcasted_iota(jnp.int32, shape, 0) // SLOT
    lanes = lax.broadcasted_iota(jnp.int32, shape, 1) // 32
    return rows == lanes


def spread_heads(block, mask):
    return jnp.where(mask, jnp.concatenate([block] * QUAD, 0), jnp.zeros((), block.dtype))


def join_heads(blocks):
    lane = lax.broadcasted_iota(jnp.int32, (SLOT, 128), 1) // 32
    out = blocks[:SLOT]
    for h in range(1, QUAD):
        out = jnp.where(lane == h, blocks[h * SLOT : (h + 1) * SLOT], out)
    return out


def attn_load(layer, info, pieces, w_in, sems, clear=()):
    mine, other = pieces[:4], pieces[4:]

    def copies(source):
        pairs = []
        for at in range(4):
            row = pl.multiple_of(jnp.bitwise_xor(info[2], at) * 128, 128)
            for c in range(3):
                src = source[at].at[128 * c : 128 * c + 128]
                pairs.append((src, w_in.at[pl.ds(row, 128), 512 * c : 512 * c + 512]))
        return [pltpu.make_async_copy(*pair, sems.at[n]) for n, pair in enumerate(pairs)]

    @pl.when(pl.program_id(0) == 0)
    def _():
        @pl.when(info[1] == layer)
        def _():
            for c in copies(mine):
                c.start()

        @pl.when(info[1] != layer)
        def _():
            for c in copies(other):
                c.start()

        for total in clear:
            total[...] = jnp.zeros(total.shape, F32)
        for c in copies(mine):
            c.wait()


def mlp_copies(info, pieces, places, sems):
    w_out, w_up, w_down = places
    copies = []
    for half_at in range(2):
        half = jnp.bitwise_xor(info[1], half_at)
        for shard_at in range(4):
            shard = jnp.bitwise_xor(info[2], shard_at)
            piece = pieces[4 * half_at + shard_at]
            row = pl.multiple_of(shard * 128 + half * 64, 64)
            deep = pl.multiple_of(shard * 512 + half * 256, 256)
            pairs = [
                (piece.at[64 * c : 64 * c + 64], w_up.at[pl.ds(row, 64), 512 * c : 512 * c + 512])
                for c in range(4)
            ]
            pairs.append((piece.at[256:512], w_down.at[pl.ds(deep, 256), :]))
            pairs.append((piece.at[512:576], w_out.at[pl.ds(row, 64), :]))
            for src, dst in pairs:
                copies.append(pltpu.make_async_copy(src, dst, sems.at[len(copies)]))
    return copies


def group_lanes(g):
    return lambda part: slice(512 * part + 128 * g, 512 * part + 128 * g + 128)


BLOCKS = [
    (w, slice(w * SLOT, w * SLOT + SLOT), g, group_lanes(g))
    for w in range(WINS)
    for g in range(GROUPS)
]


def load_weights(copies, clear=()):
    @pl.when(pl.program_id(0) == 0)
    def _():
        for c in copies:
            c.start()
        for total in clear:
            total[...] = jnp.zeros(total.shape, F32)
        for c in copies:
            c.wait()


def attn_forward_kernel(layer, info, *refs):
    pieces, refs = refs[:8], refs[8:]
    x_ref, cut_ref, join_ref, vec_ref, bias_ref, apart_ref, *refs = refs
    qkv_ref, p_ref, att_ref, w_in, sems, att = refs
    attn_load(layer, info, pieces, w_in, sems)

    @pl.when(pl.program_id(0) < info[0])
    def _():
        xhat, _ = standard(x_ref[0].astype(F32))
        normed = (xhat * vec_ref[0:1] + vec_ref[2:3]).astype(BF16)
        normed = mm(cut_ref[...], normed).astype(BF16)
        for part in range(3):
            block = mm(normed, w_in[:, 512 * part : 512 * part + 512])
            if part != 1:
                row = 3 if part == 0 else 4
                block = block + vec_ref[row : row + 1]
            qkv_ref[0, :, 512 * part : 512 * part + 512] = block.astype(BF16)
        mask = head_mask((WIDE, 128))
        factor = 32**-0.5 * LOG2E

        scores, probs, outs = [], [], []
        for w, rows, g, lanes in BLOCKS:
            q = qkv_ref[0, rows, lanes(0)]
            bias = bias_ref[g] + apart_ref[w] if layer else bias_ref[g]
            scores.append(mm_nt(qkv_ref[0, rows, lanes(1)], spread_heads(q, mask)) * factor + bias)
        for s in scores:
            e = jnp.exp2(s - jnp.max(s, 0, keepdims=True))
            probs.append((e * (1.0 / jnp.sum(e, 0, keepdims=True))).astype(BF16))
        for p, (w, rows, g, lanes) in zip(probs, BLOCKS):
            outs.append(mm_tn(p, qkv_ref[0, rows, lanes(2)]))
        for p, out, (w, rows, g, lanes) in zip(probs, outs, BLOCKS):
            p_ref[0, w, g] = p
            att[rows, lanes(0)] = join_heads(out).astype(BF16)
        att_ref[0] = mm(join_ref[...], att[...]).astype(BF16)


def mlp_forward_kernel(info, *refs):
    pieces, refs = refs[:8], refs[8:]
    x_ref, att_ref, vec_ref, up_bias_ref, *refs = refs
    out_ref, mid_ref, act_ref, slope_ref, w_out, w_up, w_down, sems = refs
    load_weights(mlp_copies(info, pieces, (w_out, w_up, w_down), sems))

    @pl.when(pl.program_id(0) < info[0])
    def _():
        mid = x_ref[0].astype(F32) + (mm(att_ref[0], w_out[...]) + vec_ref[5:6])
        mid_ref[0] = mid
        xhat, _ = standard(mid)
        normed_two = (xhat * vec_ref[1:2] + vec_ref[6:7]).astype(BF16)
        cols = [slice(512 * c, 512 * c + 512) for c in range(4)]

        def lift(c):
            return mm(normed_two, w_up[:, cols[c]]) + up_bias_ref[:, cols[c]]

        hidden, active, down = lift(0), None, 0.0
        for c in range(4):
            after = lift(c + 1) if c < 3 else None
            before, (active, slope) = active, gelu_pair(hidden)
            active = active.astype(BF16)
            act_ref[0, :, cols[c]] = active
            slope_ref[0, :, cols[c]] = slope.astype(BF16)
            if c:
                down = down + mm(before, w_down[cols[c - 1], :])
            hidden = after
        down = down + mm(active, w_down[cols[3], :])
        out_ref[0] = (mid + (down + vec_ref[7:8])).astype(BF16)


def add_row(total, at, value):
    total[at : at + 1] += jnp.sum(value, 0, keepdims=True)


def norm_back(total, rows, g_normed, xhat, inverse, gain):
    add_row(total, rows[0], g_normed * xhat)
    add_row(total, rows[1], g_normed)
    u = g_normed * gain
    lean = jnp.mean(u * xhat, -1, keepdims=True)
    return (u - jnp.mean(u, -1, keepdims=True) - xhat * lean) * inverse


def mlp_backward_kernel(info, *refs):
    pieces, refs = refs[:8], refs[8:]
    g_ref, att_ref, mid_ref, act_ref, slope_ref, vec_ref, *refs = refs
    g_mid_ref, g_att_ref, keep_ref, give_ref, vec_out, up_out, *refs = refs
    w_out, w_up, w_down, sems, d_out, d_up, d_down = refs
    load_weights(
        mlp_copies(info, pieces, (w_out, w_up, w_down), sems),
        (d_out, d_up, d_down, vec_out, up_out),
    )

    @pl.when(pl.program_id(0) < info[0])
    def _():
        g = g_ref[0]
        add_row(vec_out, 7, g.astype(F32))
        xhat, inverse = standard(mid_ref[0])
        normed_two = (xhat * vec_ref[1:2] + vec_ref[6:7]).astype(BF16)
        cols = [slice(512 * c, 512 * c + 512) for c in range(4)]
        g_hidden = []
        for c in cols:
            part = (mm_nt(g, w_down[c, :]) * slope_ref[0, :, c].astype(F32)).astype(BF16)
            up_out[:, c] += jnp.sum(part.astype(F32), 0, keepdims=True)
            g_hidden.append(part)
        g_normed = sum(mm_nt(part, w_up[:, c]) for part, c in zip(g_hidden, cols))
        for part, c in zip(g_hidden, cols):
            d_down[:, c] += mm_tn(g, act_ref[0, :, c])
            d_up[:, c] += mm_tn(normed_two, part)
        g_mid = g.astype(F32) + norm_back(vec_out, (1, 6), g_normed, xhat, inverse, vec_ref[1:2])
        g_mid_ref[0] = g_mid
        g_update = g_mid.astype(BF16)
        add_row(vec_out, 5, g_update.astype(F32))
        d_out[...] += mm_tn(att_ref[0], g_update)
        g_att_ref[0] = mm_nt(g_update, w_out[...]).astype(BF16)

    @pl.when(pl.program_id(0) == pl.num_programs(0) - 1)
    def _():
        for out_ref, half in ((keep_ref, info[1]), (give_ref, 1 - info[1])):
            for shard in range(4):
                at = jnp.bitwise_xor(info[2], shard)
                rows = pl.ds(pl.multiple_of(128 * shard + 64 * half, 64), 64)
                for c in range(4):
                    out_ref[at, 64 * c : 64 * c + 64, :] = d_up[
                        rows, 512 * c : 512 * c + 512
                    ].astype(BF16)
                deep = pl.ds(pl.multiple_of(512 * shard + 256 * half, 256), 256)
                out_ref[at, 256:512, :] = d_down[:, deep].T.astype(BF16)
                out_ref[at, 512:576, :] = d_out[rows, :].astype(BF16)


def attn_backward_kernel(layer, info, *refs):
    pieces, refs = refs[:8], refs[8:]
    g_mid_ref, g_att_ref, x_ref, qkv_ref, p_ref, cut_ref, join_ref, vec_ref, *refs = refs
    gx_ref, keep_ref, give_ref, vec_out, table_out, *refs = refs
    w_in, sems, d_in, g_att, gqkv = refs
    attn_load(layer, info, pieces, w_in, sems, (d_in, vec_out, table_out))

    @pl.when(pl.program_id(0) < info[0])
    def _():
        g_att[...] = mm(cut_ref[...], g_att_ref[0]).astype(BF16)
        mask = head_mask((WIDE, 128))

        at = range(len(BLOCKS))
        q, k, v = [[qkv_ref[0, rows, lanes(n)] for _, rows, _, lanes in BLOCKS] for n in range(3)]
        p = [p_ref[0, w, h] for w, _, h, _ in BLOCKS]
        g_out = [spread_heads(g_att[rows, lanes(0)], mask) for _, rows, _, lanes in BLOCKS]
        g_p = [mm_nt(v[n], g_out[n]) for n in at]
        g_v = [mm(p[n], g_out[n]) for n in at]
        g_s = []
        for n in at:
            soft = p[n].astype(F32)
            part = soft * g_p[n]
            g_s.append((part - soft * jnp.sum(part, 0, keepdims=True)).astype(BF16))
        g_k = [mm(g_s[n], spread_heads(q[n], mask)) for n in at]
        g_q = [mm_tn(g_s[n], k[n]) for n in at]
        for n, (_, rows, _, lanes) in enumerate(BLOCKS):
            gqkv[rows, lanes(0)] = (join_heads(g_q[n]) * 32**-0.5).astype(BF16)
            gqkv[rows, lanes(1)] = (g_k[n] * 32**-0.5).astype(BF16)
            gqkv[rows, lanes(2)] = g_v[n].astype(BF16)
        for h in range(GROUPS):
            table_out[h] += sum(g_s[n].astype(F32) for n in at if BLOCKS[n][2] == h)
        xhat, inverse = standard(x_ref[0].astype(F32))
        normed = (xhat * vec_ref[0:1] + vec_ref[2:3]).astype(BF16)
        g_normed = None
        for part in range(3):
            cols = slice(512 * part, 512 * part + 512)
            block = mm(join_ref[...], gqkv[:, cols]).astype(BF16)
            d_in[:, cols] += mm_tn(normed, block)
            if part != 1:
                add_row(vec_out, 3 if part == 0 else 4, block.astype(F32))
            term = mm_nt(block, w_in[:, cols])
            g_normed = term if g_normed is None else g_normed + term
        back = norm_back(vec_out, (0, 2), g_normed, xhat, inverse, vec_ref[0:1])
        gx_ref[0] = (g_mid_ref[0] + back).astype(BF16)

    @pl.when(pl.program_id(0) == pl.num_programs(0) - 1)
    def _():
        for out_ref, half in ((keep_ref, info[1]), (give_ref, 1 - info[1])):
            for shard in range(4):
                at = jnp.bitwise_xor(info[2], shard)
                rows = pl.ds(pl.multiple_of(128 * shard + 64 * half, 64), 64)
                for c in range(3):
                    out_ref[at, 64 * c : 64 * c + 64, :] = d_in[
                        rows, 512 * c : 512 * c + 512
                    ].astype(BF16)


def whole(shape):
    return pl.BlockSpec(shape, lambda i, info: (0,) * len(shape))


def each(shape):
    return pl.BlockSpec(
        (1,) + shape,
        lambda i, info: (jnp.maximum(jnp.minimum(i, info[0] - 1), 0),) + (0,) * len(shape),
    )


X = ((FRAME, 512), BF16)
QKV = ((ROWS, 1536), BF16)
PROB = ((WINS, GROUPS, SLOT, WIDE), BF16)
MID = ((FRAME, 512), F32)
WIDE_X = ((FRAME, 2048), BF16)
VEC = ((8, 512), F32)
ATTN_WEIGHTS = [pltpu.VMEM((512, 1536), BF16), pltpu.SemaphoreType.DMA((12,))]
MLP_WEIGHTS = [
    pltpu.VMEM((512, 512), BF16),
    pltpu.VMEM((512, 2048), BF16),
    pltpu.VMEM((2048, 512), BF16),
    pltpu.SemaphoreType.DMA((48,)),
]


def run(kernel, info, pieces, by_image, shared, outs, shared_outs, scratch, micros):
    count = by_image[0].shape[0]
    return pl.pallas_call(
        kernel,
        grid_spec=pltpu.PrefetchScalarGridSpec(
            num_scalar_prefetch=1,
            grid=(count,),
            in_specs=[pl.BlockSpec(memory_space=pl.ANY)] * len(pieces)
            + [each(a.shape[1:]) for a in by_image]
            + [whole(a.shape) for a in shared],
            out_specs=[each(shape) for shape, _ in outs]
            + [whole(shape) for shape, _ in shared_outs],
            scratch_shapes=scratch,
        ),
        out_shape=[jax.ShapeDtypeStruct((count,) + shape, kind) for shape, kind in outs]
        + [jax.ShapeDtypeStruct(shape, kind) for shape, kind in shared_outs],
        compiler_params=pltpu.CompilerParams(vmem_limit_bytes=56 * 1024 * 1024),
        cost_estimate=pl.CostEstimate(
            flops=int(micros * 1e9), bytes_accessed=int(micros * 1e6), transcendentals=0
        ),
    )(info, *pieces, *by_image, *shared)


def attn_forward(layer, info, pieces, x, cut, join, vec, bias, apart):
    return run(
        functools.partial(attn_forward_kernel, layer),
        info,
        pieces,
        [x],
        [cut, join, vec, bias, apart],
        [QKV, PROB, X],
        [],
        ATTN_WEIGHTS + [pltpu.VMEM((ROWS, 512), BF16)],
        20,
    )


def mlp_forward(info, pieces, x, att, vec, up_bias):
    return run(
        mlp_forward_kernel,
        info,
        pieces,
        [x, att],
        [vec, up_bias],
        [X, MID, WIDE_X, WIDE_X],
        [],
        MLP_WEIGHTS,
        20,
    )


def mlp_backward(info, pieces, g, att, mid, act, slope, vec):
    return run(
        mlp_backward_kernel,
        info,
        pieces,
        [g, att, mid, act, slope],
        [vec],
        [MID, X],
        [((4, 576, 512), BF16)] * 2 + [VEC, ((1, 2048), F32)],
        MLP_WEIGHTS
        + [pltpu.VMEM((512, 512), F32), pltpu.VMEM((512, 2048), F32), pltpu.VMEM((512, 2048), F32)],
        30,
    )


def attn_backward(layer, info, pieces, g_mid, g_att, x, qkv, p, cut, join, vec):
    return run(
        functools.partial(attn_backward_kernel, layer),
        info,
        pieces,
        [g_mid, g_att, x, qkv, p],
        [cut, join, vec],
        [X],
        [((4, 192, 512), BF16)] * 2 + [VEC, ((GROUPS, SLOT, WIDE), F32)],
        ATTN_WEIGHTS
        + [
            pltpu.VMEM((512, 1536), F32),
            pltpu.VMEM((ROWS, 512), BF16),
            pltpu.VMEM((ROWS, 1536), BF16),
        ],
        30,
    )


def swap(block):
    return lax.ppermute(block, "section", [(0, 1), (1, 0)])


def across(block, distance):
    return lax.ppermute(block, "shard", [(i, i ^ distance) for i in range(4)])


def along(block, distance):
    size = lax.axis_size("replica")
    return lax.ppermute(block, "replica", [(i, i ^ distance) for i in range(size)])


def tie(*values):
    return lax.optimization_barrier(values)


def by_distance(stack, at):
    for bit in (1, 2):
        other = jnp.stack([stack[d ^ bit] for d in range(4)])
        stack = jnp.where(at & bit != 0, other, stack)
    return stack


def gather_direct(own):
    return [own] + [across(own, d) for d in (1, 2, 3)]


def with_other(pieces):
    return pieces + [swap(piece) for piece in pieces]


def add_low(*terms):
    total = terms[0].astype(F32)
    for term in terms[1:]:
        total = total + term.astype(F32)
    return total.astype(BF16)


def reduce_steps(keep, give, quick):
    (got,) = yield [swap(give)]
    total = add_low(keep, got)
    got = yield [across(total[d], d) for d in (1, 2, 3)]
    owned = add_low(total[0], *got)
    size = lax.axis_size("replica")
    if size != 4:
        return lax.psum(owned, "replica")
    if quick:
        for d in (1, 2):
            (got,) = yield [along(owned, d)]
            owned = add_low(owned, got)
        return owned
    at = lax.axis_index("replica")
    quarters = owned.reshape(4, -1, 512)

    def pick(d):
        return lax.dynamic_index_in_dim(quarters, at ^ d, 0, keepdims=False)

    got = yield [along(pick(d), d) for d in (1, 2, 3)]
    total = add_low(pick(0), *got)
    got = yield [along(total, d) for d in (1, 2, 3)]
    held = jnp.stack([total] + list(got))
    return by_distance(held, at).reshape(owned.shape)


def sum_steps(block):
    (got,) = yield [swap(block)]
    block = block + got
    got = yield [across(block, d) for d in (1, 2, 3)]
    block = block + got[0] + got[1] + got[2]
    if lax.axis_size("replica") != 4:
        return lax.psum(block, "replica")
    got = yield [along(block, d) for d in (1, 2, 3)]
    return block + got[0] + got[1] + got[2]


class Flow:
    def __init__(self, steps):
        self.steps = steps
        self.sent = next(steps)
        self.total = None

    def take(self, sent):
        if self.total is None:
            try:
                self.sent = self.steps.send(list(sent))
            except StopIteration as end:
                self.total, self.sent = end.value, []


def boundary_of(values, flows):
    values, sent = tie(values, [flow.sent for flow in flows])
    for flow, block in zip(flows, sent):
        flow.take(block)
    return values


def body(
    boundary,
    norm_gains,
    biases,
    up_bias,
    offset_table,
    attention_in,
    attention_out,
    up_weight,
    down_weight,
    offset_index,
    regions,
    micro_counts,
):
    core = lax.axis_index("section")
    first = core == 0
    me = lax.axis_index("shard")
    mb_count, per_device = boundary.shape[1], boundary.shape[2]
    slots = mb_count * per_device
    share = (slots + 1) // 2

    present = (jnp.arange(per_device)[None] < micro_counts[:, None]).reshape(slots)
    rank = jnp.cumsum(present.astype(jnp.int32)) - 1
    owner = jnp.bitwise_and(rank, 1)
    place = jnp.right_shift(rank, 1)

    def slots_of(whose):
        hit = present & (owner == whose)
        hit = hit[None] & (place[None] == jnp.arange(share)[:, None])
        return jnp.sum(jnp.where(hit, jnp.arange(slots)[None], 0), 1)

    total_images = jnp.sum(present.astype(jnp.int32))
    own_count = jnp.right_shift(total_images + 1 - core, 1)
    info = jnp.stack([own_count, core, me]).astype(jnp.int32)

    flat = jnp.concatenate(
        [
            norm_gains[0].reshape(-1),
            biases[0].reshape(-1),
            up_bias[0].reshape(-1),
            offset_table[0].reshape(-1),
        ]
    )
    flat = jnp.pad(flat, (0, -flat.shape[0] % 1024)).reshape(-1, 128)

    def columns(weight):
        rows, cols = weight.shape
        return weight.reshape(2, rows // 2, cols // 512, 512).transpose(0, 2, 1, 3).reshape(2, -1, 512)

    attn_own = attention_in[0].reshape(128, 3, 512).transpose(1, 0, 2).reshape(384, 512)
    attn_own, up_weight, down_weight, attention_out, flat, boundary = tie(
        attn_own, up_weight, down_weight, attention_out, flat, boundary
    )
    attn_mine = gather_direct(attn_own)
    attn_pieces = with_other(attn_mine)
    parts = jnp.concatenate(
        [
            columns(up_weight[0]),
            down_weight[0].reshape(2, 256, 512),
            attention_out[0].reshape(2, 64, 512),
        ],
        1,
    )
    keep, got = jnp.where(first, parts[0], parts[1]), swap(jnp.where(first, parts[1], parts[0]))
    mlp_own = [jnp.where(core == layer, keep, got) for layer in range(2)]
    mlp_first, _ = tie(mlp_own[0], attn_mine[1])
    mlp_mine = gather_direct(mlp_first)

    framed = boundary.reshape(slots, TOKENS, 512)
    framed = jnp.pad(framed, ((0, 0), (0, FRAME - TOKENS), (0, 0)))
    kept = framed[slots_of(core)]
    other = swap(framed[slots_of(1 - core)])
    images = jnp.where(first, kept, other)
    cotangents = jnp.where(first, other, kept)

    small = by_distance(jnp.stack([flat] + [across(flat, d) for d in (1, 2, 3)]), me)
    small_other = swap(small)
    small = jnp.stack([jnp.where(first, small, small_other), jnp.where(first, small_other, small)])
    small = small.reshape(2, 4, -1).astype(F32)
    rel = offset_table.shape[1]
    gains = small[:, :, 0:256].reshape(2, 4, 2, 128).transpose(0, 2, 1, 3).reshape(2, 2, 512)
    shifts = small[:, :, 256:1024].reshape(2, 4, 6, 128).transpose(0, 2, 1, 3).reshape(2, 6, 512)
    vecs = jnp.concatenate([gains, shifts], 1)
    lifts = small[:, :, 1024:1536].reshape(2, 1, 2048)
    tables = small[:, :, 1536 : 1536 + 4 * rel].reshape(2, 4, rel, 4).transpose(0, 2, 1, 3).reshape(2, rel, HEADS)

    spare = SLOT - LEN
    pairs = jnp.pad(offset_index.T, ((0, spare), (0, spare))).reshape(-1)
    onehot = (pairs[None, :] == jnp.arange(rel)[:, None]).astype(BF16)
    heads_first = tables.transpose(0, 2, 1).reshape(2 * HEADS, rel).astype(BF16)
    offsets = jnp.dot(heads_first, onehot, preferred_element_type=F32)
    offsets = offsets.reshape(2, GROUPS, QUAD, SLOT, SLOT).transpose(0, 1, 3, 2, 4)
    offsets = offsets.reshape(2, GROUPS, SLOT, WIDE)
    bias = jnp.where(jnp.arange(SLOT)[:, None] < LEN, offsets * LOG2E, -1e30)
    split = regions.reshape(2, WIN, 2, WIN).transpose(0, 2, 1, 3).reshape(WINS, LEN)
    split = jnp.pad(split, ((0, 0), (0, spare)))
    apart = jnp.where(split[:, :, None] == jnp.tile(split, (1, QUAD))[:, None, :], 0.0, -100.0 * LOG2E)
    apart = apart.astype(F32)

    cut = [jnp.asarray(window_place(shift), BF16) for shift in (0, SHIFT)]
    x, saved = images, []
    for layer in range(2):
        vec = vecs[layer]
        qkv, p, att = attn_forward(
            layer, info, attn_pieces, x, cut[layer], cut[layer].T, vec, bias[layer], apart
        )
        if layer == 0:
            att, mlp_mine, mlp_second = tie(att, mlp_mine, mlp_own[1])
            mlp_pieces = [with_other(mlp_mine)]
            mlp_mine = gather_direct(mlp_second)
        out, mid, act, slope = mlp_forward(info, mlp_pieces[layer], x, att, vec, lifts[layer])
        if layer == 0:
            out, mlp_mine = tie(out, mlp_mine)
            mlp_pieces.append(with_other(mlp_mine))
        saved.append((x, qkv, p, att, mid, act, slope))
        x = out
    output, g = x, cotangents
    small_sums = [None, None]

    def backward_mlp(layer, g):
        x, qkv, p, att, mid, act, slope = saved[layer]
        return mlp_backward(info, mlp_pieces[layer], g, att, mid, act, slope, vecs[layer])

    def backward_attn(layer, g_mid, g_att):
        x, qkv, p, *_ = saved[layer]
        return attn_backward(
            layer,
            info,
            attn_pieces,
            g_mid,
            g_att,
            x,
            qkv,
            p,
            cut[layer],
            cut[layer].T,
            vecs[layer],
        )

    def small_of(vec, up, table):
        table = table.reshape(GROUPS, SLOT, QUAD, SLOT).transpose(0, 2, 1, 3)
        table = table.reshape(HEADS, SLOT * SLOT)
        table = lax.dot_general(
            table, onehot.astype(F32), (((1,), (1,)), ((), ())), precision=lax.Precision.HIGHEST
        )
        return jnp.concatenate([vec.reshape(-1), up.reshape(-1), table.reshape(-1)])

    g_mid, g_att, *sums, mlp_vec, up_sums = backward_mlp(1, g)
    second_mlp = Flow(reduce_steps(*sums, False))
    g_mid, g_att = boundary_of((g_mid, g_att), [second_mlp])
    g, *sums, attn_vec, table = backward_attn(1, g_mid, g_att)
    second_small = (mlp_vec + attn_vec, up_sums, table)
    g, sums = boundary_of((g, sums), [second_mlp])
    second_attn = Flow(reduce_steps(*sums, True))
    g = boundary_of(g, [second_attn])
    g_mid, g_att, *sums, mlp_vec, up_sums = backward_mlp(0, g)
    second_small = small_of(*second_small)
    g_mid, g_att, sums, second_small = boundary_of(
        (g_mid, g_att, sums, second_small), [second_mlp, second_attn]
    )
    first_mlp = Flow(reduce_steps(*sums, False))
    g_mid, g_att = boundary_of((g_mid, g_att), [first_mlp])
    g, *sums, attn_vec, table = backward_attn(0, g_mid, g_att)
    first_attn = Flow(reduce_steps(*sums, True))
    g = boundary_of(g, [second_mlp, second_attn, first_mlp])
    hold = jnp.where(first, g, output)
    back = swap(jnp.where(first, output, g))
    small = jnp.stack([small_of(mlp_vec + attn_vec, up_sums, table), second_small])
    width = small.shape[1]
    small = jnp.pad(small, ((0, 0), (0, -width % 1024))).reshape(-1, 128)
    back, small = boundary_of((back, small), [first_attn])
    small_flow = Flow(sum_steps(small))

    every = jnp.concatenate([hold, back], 0)
    source = jnp.clip(jnp.where(owner == core, 0, share) + place, 0, 2 * share - 1)
    chosen = every[source][:, :TOKENS]
    chosen = jnp.where(present[:, None, None], chosen, jnp.zeros((), BF16))
    results = chosen.reshape(1, mb_count, per_device, SIDE, SIDE, 512)
    results = boundary_of(results, [first_attn, small_flow, first_mlp, second_attn])
    flows = [first_attn, small_flow, second_attn, first_mlp, second_mlp]
    while any(flow.total is None for flow in flows[1:]):
        boundary_of((), flows)

    def exchanged(one, two):
        hold = jnp.where(first, one, two)
        back = swap(jnp.where(first, two, one))
        return jnp.stack([jnp.where(first, hold, back), jnp.where(first, back, hold)])

    mlp = exchanged(first_mlp.total, second_mlp.total)
    while first_attn.total is None:
        (mlp,) = boundary_of((mlp,), [first_attn])
    mlp = mlp.astype(F32)
    attn = exchanged(first_attn.total, second_attn.total).astype(F32)
    grad_in = attn.reshape(2, 3, 64, 512).transpose(0, 2, 1, 3).reshape(128, 1536)
    grad_up = mlp[:, 0:256].reshape(2, 4, 64, 512).transpose(0, 2, 1, 3).reshape(128, 2048)
    grad_down = mlp[:, 256:512].reshape(512, 512)
    grad_out = mlp[:, 512:576].reshape(128, 512)

    bundle = small_flow.total.reshape(2, -1)[:, :width]
    bundle = lax.dynamic_index_in_dim(bundle, core, 0, keepdims=False)
    vec = lax.dynamic_slice_in_dim(bundle[:4096].reshape(8, 512), me * 128, 128, 1)
    grad_lift = lax.dynamic_slice_in_dim(bundle[4096:6144], me * 512, 512, 0)
    grad_table = lax.dynamic_slice_in_dim(bundle[6144:].reshape(HEADS, rel), me * 4, 4, 0).T

    return (
        results,
        vec[None, 0:2],
        vec[None, 2:8],
        grad_lift[None],
        grad_table[None],
        grad_in[None],
        grad_out[None],
        grad_up[None],
        grad_down[None],
    )


def solution(mesh):
    placed = (
        P("section", None, ("shard", "replica"), None, None, None),
        P("section", None, "shard"),
        P("section", None, "shard"),
        P("section", "shard"),
        P("section", None, "shard"),
        P("section", "shard", None),
        P("section", "shard", None),
        P("section", "shard", None),
        P("section", "shard", None),
        P(),
        P(),
        P(),
    )
    return jax.shard_map(
        body,
        mesh=mesh,
        in_specs=placed,
        out_specs=(placed[0],) + placed[1:9],
        check_vma=False,
    )
```

profile of v0, /device:TPU:0, one launch (start us, length us, event | category | flops | bytes accessed | tf_op | source)
XLA Modules:
  0.0 383.0 jit_solution(13901418017157451026)
XLA Ops:
  5.3 3.0 collective-permute-start.10
  9.8 2.9 collective-permute-start.2
  22.9 2.3 copy.70
  25.2 2.7 reshape.346
  28.0 3.6 gather_fusion.1
  33.3 2.4 gather.18
  42.4 2.9 collective-permute-start.15
  45.3 3.3 broadcast_select_fusion.2
  50.4 14.3 %shard_map.205 = (bf16[6,256,1536]{2,1,0:T(8,128)(2,1)}, bf16[6,4,4,64,256]{4,3,2,1,0:T(8,128)(2,1)}, bf16[6,208,512]{2,1,0:T(8,128)(2,1)}) custom-call(s32[3]{0:T(128)} %pad_add_fusion.info, bf16[384,512]{1,0:T(8,128)(2,1)} %bitcast.5.refs_0_, bf16[384,512]{1,0:T(8,128)(2,1)} %collective-permute-done.refs_1_, ...), custom_call_target="tpu_custom_call" | custom-call | flops 20000000000 | bytes 20000000 | tf_op jit(solution)/shard_map/pallas_call | solution.py:377
  64.6 7.2 %collective-permute-done.14.refs_2_ = bf16[576,512]{1,0:T(8,128)(2,1)S(1)} collective-permute-done((bf16[576,512]{1,0:T(8,128)(2,1)S(1)}, bf16[576,512]{1,0:T(8,128)(2,1)S(1)}, u32[]{:S(2)}, u32[]{:S(2)}) %collective-permute-start.14) | collective-permute-done | bytes 589856 | tf_op jit(solution)/shard_map/ppermute | solution.py:465
  74.4 2.4 collective-permute-start.22
  79.0 18.9 %shard_map.206 = (bf16[6,208,512]{2,1,0:T(8,128)(2,1)}, f32[6,208,512]{2,1,0:T(8,128)}, bf16[6,208,2048]{2,1,0:T(8,128)(2,1)}, bf16[6,208,2048]{2,1,0:T(8,128)(2,1)}) custom-call(s32[3]{0:T(128)} %pad_add_fusion.info, bf16[576,512]{1,0:T(8,128)(2,1)} %copy-done.13, bf16[576,512]{1,0:T(8,128)(2,1)} %copy-done.30, bf16[576,512]{1,0:T(8,128)(2,1)} %copy-done.29, ...), custom_call_target="tpu_custom_call" | custom-call | flops 20000000000 | bytes 20000000 | tf_op jit(solution)/shard_map/pallas_call | solution.py:377
  97.9 5.4 %collective-permute-done.21.refs_2_ = bf16[576,512]{1,0:T(8,128)(2,1)S(1)} collective-permute-done((bf16[576,512]{1,0:T(8,128)(2,1)S(1)}, bf16[576,512]{1,0:T(8,128)(2,1)S(1)}, u32[]{:S(2)}, u32[]{:S(2)}) %collective-permute-start.21) | collective-permute-done | bytes 589856 | tf_op jit(solution)/shard_map/ppermute | solution.py:465
  104.4 14.3 %shard_map.207 = (bf16[6,256,1536]{2,1,0:T(8,128)(2,1)}, bf16[6,4,4,64,256]{4,3,2,1,0:T(8,128)(2,1)}, bf16[6,208,512]{2,1,0:T(8,128)(2,1)}) custom-call(s32[3]{0:T(128)} %pad_add_fusion.info, bf16[384,512]{1,0:T(8,128)(2,1)} %bitcast.5.refs_0_, bf16[384,512]{1,0:T(8,128)(2,1)} %collective-permute-done.refs_1_, ...), custom_call_target="tpu_custom_call" | custom-call | flops 20000000000 | bytes 20000000 | tf_op jit(solution)/shard_map/pallas_call | solution.py:377
  120.1 19.0 %shard_map.208 = (bf16[6,208,512]{2,1,0:T(8,128)(2,1)}, f32[6,208,512]{2,1,0:T(8,128)}, bf16[6,208,2048]{2,1,0:T(8,128)(2,1)}, bf16[6,208,2048]{2,1,0:T(8,128)(2,1)}) custom-call(s32[3]{0:T(128)} %pad_add_fusion.info, bf16[576,512]{1,0:T(8,128)(2,1)} %copy-done.14, bf16[576,512]{1,0:T(8,128)(2,1)} %copy-done.37, bf16[576,512]{1,0:T(8,128)(2,1)} %copy-done.36, ...), custom_call_target="tpu_custom_call" | custom-call | flops 20000000000 | bytes 20000000 | tf_op jit(solution)/shard_map/pallas_call | solution.py:377
  139.2 24.4 %shard_map.209 = (f32[6,208,512]{2,1,0:T(8,128)}, bf16[6,208,512]{2,1,0:T(8,128)(2,1)}, bf16[4,576,512]{2,1,0:T(8,128)(2,1)}, bf16[4,576,512]{2,1,0:T(8,128)(2,1)}, f32[8,512]{1,0:T(8,128)}, /*index=5*/f32[1,2048]{1,0:T(1,128)}) custom-call(s32[3]{0:T(128)} %pad_add_fusion.info, bf16[576,512]{1,0:T(8,128)(2,1)} %copy-done.14, bf16[576,512]{1,0:T(8,128)(2,1)} %copy-done.37, ...), custom_call_target="tpu_custom_call" | custom-call | flops 30000001024 | bytes 30000000 | tf_op jit(solution)/shard_map/pallas_call | solution.py:377
  163.7 4.6 %collective-permute-done.27 = bf16[4,576,512]{2,1,0:T(8,128)(2,1)S(1)} collective-permute-done((bf16[4,576,512]{2,1,0:T(8,128)(2,1)}, bf16[4,576,512]{2,1,0:T(8,128)(2,1)S(1)}, u32[]{:S(2)}, u32[]{:S(2)}) %collective-permute-start.27) | collective-permute-done | bytes 2359328 | tf_op jit(solution)/shard_map/ppermute | solution.py:461
  169.8 3.1 add_convert_fusion.1
  174.2 1.7 collective-permute-start.30
  177.7 21.7 %shard_map.210 = (bf16[6,208,512]{2,1,0:T(8,128)(2,1)}, bf16[4,192,512]{2,1,0:T(8,128)(2,1)}, bf16[4,192,512]{2,1,0:T(8,128)(2,1)}, f32[8,512]{1,0:T(8,128)}, f32[4,64,256]{2,1,0:T(8,128)}) custom-call(s32[3]{0:T(128)} %pad_add_fusion.info, bf16[384,512]{1,0:T(8,128)(2,1)} %bitcast.5.refs_0_, bf16[384,512]{1,0:T(8,128)(2,1)} %collective-permute-done.refs_1_, ...), custom_call_target="tpu_custom_call" | custom-call | flops 30000001024 | bytes 30000000 | tf_op jit(solution)/shard_map/pallas_call | solution.py:377
  201.6 1.9 collective-permute-done.29
  206.8 3.7 collective-permute-start.34
  216.9 24.4 %shard_map.211 = (f32[6,208,512]{2,1,0:T(8,128)}, bf16[6,208,512]{2,1,0:T(8,128)(2,1)}, bf16[4,576,512]{2,1,0:T(8,128)(2,1)}, bf16[4,576,512]{2,1,0:T(8,128)(2,1)}, f32[8,512]{1,0:T(8,128)}, /*index=5*/f32[1,2048]{1,0:T(1,128)}) custom-call(s32[3]{0:T(128)} %pad_add_fusion.info, bf16[576,512]{1,0:T(8,128)(2,1)} %copy-done.13, bf16[576,512]{1,0:T(8,128)(2,1)} %copy-done.30, ...), custom_call_target="tpu_custom_call" | custom-call | flops 30000001024 | bytes 30000000 | tf_op jit(solution)/shard_map/pallas_call | solution.py:377
  242.2 3.7 collective-permute-start.41
  245.9 3.8 collective-permute-start.40
  251.1 3.1 add_convert_fusion
  259.0 21.7 %shard_map.212 = (bf16[6,208,512]{2,1,0:T(8,128)(2,1)}, bf16[4,192,512]{2,1,0:T(8,128)(2,1)}, bf16[4,192,512]{2,1,0:T(8,128)(2,1)}, f32[8,512]{1,0:T(8,128)}, f32[4,64,256]{2,1,0:T(8,128)}) custom-call(s32[3]{0:T(128)} %pad_add_fusion.info, bf16[384,512]{1,0:T(8,128)(2,1)} %bitcast.5.refs_0_, bf16[384,512]{1,0:T(8,128)(2,1)} %collective-permute-done.refs_1_, ...), custom_call_target="tpu_custom_call" | custom-call | flops 30000001024 | bytes 30000000 | tf_op jit(solution)/shard_map/pallas_call | solution.py:377
  283.4 2.1 fusion.3
  288.6 2.3 collective-permute-done.39
  290.9 2.1 collective-permute-done.42
  293.0 3.4 broadcast_select_fusion.1
  298.4 2.2 collective-permute-start.55
  305.5 2.1 maximum_select_fusion.2
  307.5 2.1 collective-permute-start.52
  311.4 2.4 gather_fusion.2
  316.1 7.3 %collective-permute-done.53 = bf16[144,512]{1,0:T(8,128)(2,1)} collective-permute-done((bf16[144,512]{1,0:T(8,128)(2,1)}, bf16[144,512]{1,0:T(8,128)(2,1)}, u32[]{:S(2)}, u32[]{:S(2)}) %collective-permute-start.53) | collective-permute-done | bytes 147488 | tf_op jit(solution)/shard_map/ppermute | solution.py:470
  325.4 3.4 slice_select_fusion
  328.8 2.7 reshape.366
  337.2 2.5 collective-permute-start.62
  341.0 2.0 collective-permute-start.60
  344.2 3.7 copy.85
  347.9 3.7 collective-permute-done.61
  351.7 2.1 collective-permute-done.56
  353.8 2.4 collective-permute-start.66
  356.2 2.0 collective-permute-start.64
  359.5 1.8 broadcast_select_fusion.5
  361.3 5.6 %collective-permute-done.65 = f32[144,128]{1,0:T(8,128)S(1)} collective-permute-done((f32[144,128]{1,0:T(8,128)S(1)}, f32[144,128]{1,0:T(8,128)S(1)}, u32[]{:S(2)}, u32[]{:S(2)}) %collective-permute-start.65) | collective-permute-done | bytes 73760 | tf_op jit(solution)/shard_map/ppermute | solution.py:470
  367.0 3.4 collective-permute-done.63
  (330 shorter events, 96.0 us)
Async XLA Ops:
  5.3 16.1 %collective-permute-start.10 = (bf16[24,128]{1,0:T(8,128)(2,1)S(1)}, bf16[24,128]{1,0:T(8,128)(2,1)S(1)}, u32[]{:S(2)}, u32[]{:S(2)}) collective-permute-start(bf16[24,128]{1,0:T(8,128)(2,1)S(1)} %fusion.44), channel_id=1, source_target_pairs={{0,8},{4,12},{8,0},{12,4},{1,9},{5,13},{9,1},{13,5},{2,10},{6,14},... | collective-permute-start | bytes 18440 | tf_op jit(solution)/shard_map/ppermute | solution.py:465
  8.3 13.3 %collective-permute-start.9 = (bf16[24,128]{1,0:T(8,128)(2,1)S(1)}, bf16[24,128]{1,0:T(8,128)(2,1)S(1)}, u32[]{:S(2)}, u32[]{:S(2)}) collective-permute-start(bf16[24,128]{1,0:T(8,128)(2,1)S(1)} %fusion.44), channel_id=1, source_target_pairs={{0,12},{4,8},{8,4},{12,0},{1,13},{5,9},{9,5},{13,1},{2,14},{6,10},... | collective-permute-start | bytes 18440 | tf_op jit(solution)/shard_map/ppermute | solution.py:465
  9.7 11.8 %collective-permute-start.8 = (bf16[24,128]{1,0:T(8,128)(2,1)S(1)}, bf16[24,128]{1,0:T(8,128)(2,1)S(1)}, u32[]{:S(2)}, u32[]{:S(2)}) collective-permute-start(bf16[24,128]{1,0:T(8,128)(2,1)S(1)} %fusion.44), channel_id=1, source_target_pairs={{0,4},{4,0},{8,12},{12,8},{1,5},{5,1},{9,13},{13,9},{2,6},{6,2},{1... | collective-permute-start | bytes 18440 | tf_op jit(solution)/shard_map/ppermute | solution.py:465
  9.8 30.2 %collective-permute-start.2 = (bf16[384,512]{1,0:T(8,128)(2,1)}, bf16[384,512]{1,0:T(8,128)(2,1)}, u32[]{:S(2)}, u32[]{:S(2)}) collective-permute-start(bf16[384,512]{1,0:T(8,128)(2,1)} %bitcast.5.refs_0_), channel_id=1, source_target_pairs={{0,12},{4,8},{8,4},{12,0},{1,13},{5,9},{9,5},{13,1},{2,14},{6,10},... | collective-permute-start | bytes 1179656 | tf_op jit(solution)/shard_map/ppermute | solution.py:465
  12.7 27.8 %collective-permute-start.1 = (bf16[384,512]{1,0:T(8,128)(2,1)}, bf16[384,512]{1,0:T(8,128)(2,1)}, u32[]{:S(2)}, u32[]{:S(2)}) collective-permute-start(bf16[384,512]{1,0:T(8,128)(2,1)} %bitcast.5.refs_0_), channel_id=1, source_target_pairs={{0,8},{4,12},{8,0},{12,4},{1,9},{5,13},{9,1},{13,5},{2,10},{6,14},... | collective-permute-start | bytes 1179656 | tf_op jit(solution)/shard_map/ppermute | solution.py:465
  21.4 19.3 %collective-permute-start = (bf16[384,512]{1,0:T(8,128)(2,1)}, bf16[384,512]{1,0:T(8,128)(2,1)}, u32[]{:S(2)}, u32[]{:S(2)}) collective-permute-start(bf16[384,512]{1,0:T(8,128)(2,1)} %bitcast.5.refs_0_), channel_id=1, source_target_pairs={{0,4},{4,0},{8,12},{12,8},{1,5},{5,1},{9,13},{13,9},{2,6},{6,2},{1... | collective-permute-start | bytes 1179656 | tf_op jit(solution)/shard_map/ppermute | solution.py:465
  21.6 19.5 %collective-permute-start.12 = (bf16[576,512]{1,0:T(8,128)(2,1)}, bf16[576,512]{1,0:T(8,128)(2,1)}, u32[]{:S(2)}, u32[]{:S(2)}) collective-permute-start(bf16[576,512]{1,0:T(8,128)(2,1)} %select_bitcast_fusion), channel_id=1, source_target_pairs={{0,16},{16,0},{1,17},{17,1},{2,18},{18,2},{3,19},{19,3},{4,20},{20... | collective-permute-start | bytes 1769480 | tf_op jit(solution)/shard_map/ppermute | solution.py:461
  21.6 14.1 %collective-permute-start.11 = (bf16[4,24,128]{2,1,0:T(8,128)(2,1)S(1)}, bf16[4,24,128]{2,1,0:T(8,128)(2,1)S(1)}, u32[]{:S(2)}, u32[]{:S(2)}) collective-permute-start(bf16[4,24,128]{2,1,0:T(8,128)(2,1)S(1)} %maximum_select_fusion.5), channel_id=1, source_target_pairs={{0,16},{16,0},{1,17},{17,1},{2,18},{18,2},{3,19},{19,3},{4,20},{20... | collective-permute-start | bytes 73736 | tf_op jit(solution)/shard_map/ppermute | solution.py:461
  42.4 22.3 %collective-permute-start.15 = (bf16[576,512]{1,0:T(8,128)(2,1)S(1)}, bf16[576,512]{1,0:T(8,128)(2,1)S(1)}, u32[]{:S(2)}, u32[]{:S(2)}) collective-permute-start(bf16[576,512]{1,0:T(8,128)(2,1)S(1)} %get-tuple-element.127.refs_0_), channel_id=1, source_target_pairs={{0,12},{4,8},{8,4},{12,0},{1,13},{5,9},{9,5},{13,1},{2,14},{6,10},... | collective-permute-start | bytes 1769480 | tf_op jit(solution)/shard_map/ppermute | solution.py:465
  48.6 23.3 %collective-permute-start.14 = (bf16[576,512]{1,0:T(8,128)(2,1)S(1)}, bf16[576,512]{1,0:T(8,128)(2,1)S(1)}, u32[]{:S(2)}, u32[]{:S(2)}) collective-permute-start(bf16[576,512]{1,0:T(8,128)(2,1)S(1)} %get-tuple-element.127.refs_0_), channel_id=1, source_target_pairs={{0,8},{4,12},{8,0},{12,4},{1,9},{5,13},{9,1},{13,5},{2,10},{6,14},... | collective-permute-start | bytes 1769480 | tf_op jit(solution)/shard_map/ppermute | solution.py:465
  49.1 23.1 %collective-permute-start.13 = (bf16[576,512]{1,0:T(8,128)(2,1)S(1)}, bf16[576,512]{1,0:T(8,128)(2,1)S(1)}, u32[]{:S(2)}, u32[]{:S(2)}) collective-permute-start(bf16[576,512]{1,0:T(8,128)(2,1)S(1)} %get-tuple-element.127.refs_0_), channel_id=1, source_target_pairs={{0,4},{4,0},{8,12},{12,8},{1,5},{5,1},{9,13},{13,9},{2,6},{6,2},{1... | collective-permute-start | bytes 1769480 | tf_op jit(solution)/shard_map/ppermute | solution.py:465
  74.4 23.5 %collective-permute-start.22 = (bf16[576,512]{1,0:T(8,128)(2,1)S(1)}, bf16[576,512]{1,0:T(8,128)(2,1)S(1)}, u32[]{:S(2)}, u32[]{:S(2)}) collective-permute-start(bf16[576,512]{1,0:T(8,128)(2,1)S(1)} %get-tuple-element.134.refs_0_), channel_id=1, source_target_pairs={{0,12},{4,8},{8,4},{12,0},{1,13},{5,9},{9,5},{13,1},{2,14},{6,10},... | collective-permute-start | bytes 1769480 | tf_op jit(solution)/shard_map/ppermute | solution.py:465
  76.8 26.4 %collective-permute-start.21 = (bf16[576,512]{1,0:T(8,128)(2,1)S(1)}, bf16[576,512]{1,0:T(8,128)(2,1)S(1)}, u32[]{:S(2)}, u32[]{:S(2)}) collective-permute-start(bf16[576,512]{1,0:T(8,128)(2,1)S(1)} %get-tuple-element.134.refs_0_), channel_id=1, source_target_pairs={{0,8},{4,12},{8,0},{12,4},{1,9},{5,13},{9,1},{13,5},{2,10},{6,14},... | collective-permute-start | bytes 1769480 | tf_op jit(solution)/shard_map/ppermute | solution.py:465
  77.4 26.0 %collective-permute-start.20 = (bf16[576,512]{1,0:T(8,128)(2,1)S(1)}, bf16[576,512]{1,0:T(8,128)(2,1)S(1)}, u32[]{:S(2)}, u32[]{:S(2)}) collective-permute-start(bf16[576,512]{1,0:T(8,128)(2,1)S(1)} %get-tuple-element.134.refs_0_), channel_id=1, source_target_pairs={{0,4},{4,0},{8,12},{12,8},{1,5},{5,1},{9,13},{13,9},{2,6},{6,2},{1... | collective-permute-start | bytes 1769480 | tf_op jit(solution)/shard_map/ppermute | solution.py:465
  103.3 15.4 %collective-permute-start.23 = (bf16[576,512]{1,0:T(8,128)(2,1)S(1)}, bf16[576,512]{1,0:T(8,128)(2,1)S(1)}, u32[]{:S(2)}, u32[]{:S(2)}) collective-permute-start(bf16[576,512]{1,0:T(8,128)(2,1)S(1)} %get-tuple-element.134.refs_0_), channel_id=1, source_target_pairs={{0,16},{16,0},{1,17},{17,1},{2,18},{18,2},{3,19},{19,3},{4,20},{20... | collective-permute-start | bytes 1769480 | tf_op jit(solution)/shard_map/ppermute | solution.py:461
  103.3 15.4 %collective-permute-start.24 = (bf16[576,512]{1,0:T(8,128)(2,1)S(1)}, bf16[576,512]{1,0:T(8,128)(2,1)S(1)}, u32[]{:S(2)}, u32[]{:S(2)}) collective-permute-start(bf16[576,512]{1,0:T(8,128)(2,1)S(1)} %collective-permute-done.20.refs_1_), channel_id=1, source_target_pairs={{0,16},{16,0},{1,17},{17,1},{2,18},{18,2},{3,19},{19,3},{4,20},{20... | collective-permute-start | bytes 1769480 | tf_op jit(solution)/shard_map/ppermute | solution.py:461
  103.9 14.9 %collective-permute-start.25 = (bf16[576,512]{1,0:T(8,128)(2,1)S(1)}, bf16[576,512]{1,0:T(8,128)(2,1)S(1)}, u32[]{:S(2)}, u32[]{:S(2)}) collective-permute-start(bf16[576,512]{1,0:T(8,128)(2,1)S(1)} %collective-permute-done.21.refs_2_), channel_id=1, source_target_pairs={{0,16},{16,0},{1,17},{17,1},{2,18},{18,2},{3,19},{19,3},{4,20},{20... | collective-permute-start | bytes 1769480 | tf_op jit(solution)/shard_map/ppermute | solution.py:461
  103.9 14.8 %collective-permute-start.26 = (bf16[576,512]{1,0:T(8,128)(2,1)S(1)}, bf16[576,512]{1,0:T(8,128)(2,1)S(1)}, u32[]{:S(2)}, u32[]{:S(2)}) collective-permute-start(bf16[576,512]{1,0:T(8,128)(2,1)S(1)} %collective-permute-done.22.refs_3_), channel_id=1, source_target_pairs={{0,16},{16,0},{1,17},{17,1},{2,18},{18,2},{3,19},{19,3},{4,20},{20... | collective-permute-start | bytes 1769480 | tf_op jit(solution)/shard_map/ppermute | solution.py:461
  174.2 27.4 %collective-permute-start.30 = (bf16[576,512]{1,0:T(8,128)(2,1)}, bf16[576,512]{1,0:T(8,128)(2,1)}, u32[]{:S(2)}, u32[]{:S(2)}) collective-permute-start(bf16[576,512]{1,0:T(8,128)(2,1)} %get-tuple-element.276), channel_id=1, source_target_pairs={{0,12},{4,8},{8,4},{12,0},{1,13},{5,9},{9,5},{13,1},{2,14},{6,10},... | collective-permute-start | bytes 1769480 | tf_op jit(solution)/shard_map/ppermute | solution.py:465
  175.9 27.5 %collective-permute-start.29 = (bf16[576,512]{1,0:T(8,128)(2,1)}, bf16[576,512]{1,0:T(8,128)(2,1)}, u32[]{:S(2)}, u32[]{:S(2)}) collective-permute-start(bf16[576,512]{1,0:T(8,128)(2,1)} %get-tuple-element.277), channel_id=1, source_target_pairs={{0,8},{4,12},{8,0},{12,4},{1,9},{5,13},{9,1},{13,5},{2,10},{6,14},... | collective-permute-start | bytes 1769480 | tf_op jit(solution)/shard_map/ppermute | solution.py:465
  177.2 26.3 %collective-permute-start.28 = (bf16[576,512]{1,0:T(8,128)(2,1)}, bf16[576,512]{1,0:T(8,128)(2,1)}, u32[]{:S(2)}, u32[]{:S(2)}) collective-permute-start(bf16[576,512]{1,0:T(8,128)(2,1)} %get-tuple-element.278), channel_id=1, source_target_pairs={{0,4},{4,0},{8,12},{12,8},{1,5},{5,1},{9,13},{13,9},{2,6},{6,2},{1... | collective-permute-start | bytes 1769480 | tf_op jit(solution)/shard_map/ppermute | solution.py:465
  210.5 30.8 %collective-permute-start.33 = (bf16[144,512]{1,0:T(8,128)(2,1)S(1)}, bf16[144,512]{1,0:T(8,128)(2,1)S(1)}, u32[]{:S(2)}, u32[]{:S(2)}) collective-permute-start(bf16[144,512]{1,0:T(8,128)(2,1)S(1)} %get-tuple-element.301), channel_id=1, source_target_pairs={{0,2},{1,3},{2,0},{3,1},{4,6},{5,7},{6,4},{7,5},{8,10},{9,11},{10,... | collective-permute-start | bytes 442376 | tf_op jit(solution)/shard_map/ppermute | solution.py:470
  210.5 30.8 %collective-permute-start.32 = (bf16[144,512]{1,0:T(8,128)(2,1)S(1)}, bf16[144,512]{1,0:T(8,128)(2,1)S(1)}, u32[]{:S(2)}, u32[]{:S(2)}) collective-permute-start(bf16[144,512]{1,0:T(8,128)(2,1)S(1)} %get-tuple-element.302), channel_id=1, source_target_pairs={{0,1},{1,0},{2,3},{3,2},{4,5},{5,4},{6,7},{7,6},{8,9},{9,8},{10,11... | collective-permute-start | bytes 442376 | tf_op jit(solution)/shard_map/ppermute | solution.py:470
  212.9 28.4 %collective-permute-start.37 = (bf16[192,512]{1,0:T(8,128)(2,1)S(1)}, bf16[192,512]{1,0:T(8,128)(2,1)S(1)}, u32[]{:S(2)}, u32[]{:S(2)}) collective-permute-start(bf16[192,512]{1,0:T(8,128)(2,1)S(1)} %get-tuple-element.290), channel_id=1, source_target_pairs={{0,12},{4,8},{8,4},{12,0},{1,13},{5,9},{9,5},{13,1},{2,14},{6,10},... | collective-permute-start | bytes 589832 | tf_op jit(solution)/shard_map/ppermute | solution.py:465
  214.7 26.7 %collective-permute-start.36 = (bf16[192,512]{1,0:T(8,128)(2,1)S(1)}, bf16[192,512]{1,0:T(8,128)(2,1)S(1)}, u32[]{:S(2)}, u32[]{:S(2)}) collective-permute-start(bf16[192,512]{1,0:T(8,128)(2,1)S(1)} %get-tuple-element.291), channel_id=1, source_target_pairs={{0,8},{4,12},{8,0},{12,4},{1,9},{5,13},{9,1},{13,5},{2,10},{6,14},... | collective-permute-start | bytes 589832 | tf_op jit(solution)/shard_map/ppermute | solution.py:465
  215.9 25.5 %collective-permute-start.35 = (bf16[192,512]{1,0:T(8,128)(2,1)S(1)}, bf16[192,512]{1,0:T(8,128)(2,1)S(1)}, u32[]{:S(2)}, u32[]{:S(2)}) collective-permute-start(bf16[192,512]{1,0:T(8,128)(2,1)S(1)} %get-tuple-element.292), channel_id=1, source_target_pairs={{0,4},{4,0},{8,12},{12,8},{1,5},{5,1},{9,13},{13,9},{2,6},{6,2},{1... | collective-permute-start | bytes 589832 | tf_op jit(solution)/shard_map/ppermute | solution.py:465
  242.2 43.5 %collective-permute-start.41 = (bf16[144,512]{1,0:T(8,128)(2,1)S(1)}, bf16[144,512]{1,0:T(8,128)(2,1)}, u32[]{:S(2)}, u32[]{:S(2)}) collective-permute-start(bf16[144,512]{1,0:T(8,128)(2,1)S(1)} %fusion.32), channel_id=1, source_target_pairs={{0,3},{1,2},{2,1},{3,0},{4,7},{5,6},{6,5},{7,4},{8,11},{9,10},{10,... | collective-permute-start | bytes 442376 | tf_op jit(solution)/shard_map/ppermute | solution.py:470
  245.9 41.1 %collective-permute-start.40 = (bf16[144,512]{1,0:T(8,128)(2,1)S(1)}, bf16[144,512]{1,0:T(8,128)(2,1)}, u32[]{:S(2)}, u32[]{:S(2)}) collective-permute-start(bf16[144,512]{1,0:T(8,128)(2,1)S(1)} %fusion.32), channel_id=1, source_target_pairs={{0,2},{1,3},{2,0},{3,1},{4,6},{5,7},{6,4},{7,5},{8,10},{9,11},{10,... | collective-permute-start | bytes 442376 | tf_op jit(solution)/shard_map/ppermute | solution.py:470
  255.5 37.5 %collective-permute-start.45 = (bf16[576,512]{1,0:T(8,128)(2,1)}, bf16[576,512]{1,0:T(8,128)(2,1)}, u32[]{:S(2)}, u32[]{:S(2)}) collective-permute-start(bf16[576,512]{1,0:T(8,128)(2,1)} %get-tuple-element.273), channel_id=1, source_target_pairs={{0,12},{4,8},{8,4},{12,0},{1,13},{5,9},{9,5},{13,1},{2,14},{6,10},... | collective-permute-start | bytes 1769480 | tf_op jit(solution)/shard_map/ppermute | solution.py:465
  257.0 36.1 %collective-permute-start.44 = (bf16[576,512]{1,0:T(8,128)(2,1)}, bf16[576,512]{1,0:T(8,128)(2,1)}, u32[]{:S(2)}, u32[]{:S(2)}) collective-permute-start(bf16[576,512]{1,0:T(8,128)(2,1)} %get-tuple-element.274), channel_id=1, source_target_pairs={{0,8},{4,12},{8,0},{12,4},{1,9},{5,13},{9,1},{13,5},{2,10},{6,14},... | collective-permute-start | bytes 1769480 | tf_op jit(solution)/shard_map/ppermute | solution.py:465
  257.5 35.5 %collective-permute-start.43 = (bf16[576,512]{1,0:T(8,128)(2,1)}, bf16[576,512]{1,0:T(8,128)(2,1)}, u32[]{:S(2)}, u32[]{:S(2)}) collective-permute-start(bf16[576,512]{1,0:T(8,128)(2,1)} %get-tuple-element.275), channel_id=1, source_target_pairs={{0,4},{4,0},{8,12},{12,8},{1,5},{5,1},{9,13},{13,9},{2,6},{6,2},{1... | collective-permute-start | bytes 1769480 | tf_op jit(solution)/shard_map/ppermute | solution.py:465
  296.4 13.2 %collective-permute-start.46 = (bf16[6,208,512]{2,1,0:T(8,128)(2,1)}, bf16[6,208,512]{2,1,0:T(8,128)(2,1)}, u32[]{:S(2)}, u32[]{:S(2)}) collective-permute-start(bf16[6,208,512]{2,1,0:T(8,128)(2,1)} %get-tuple-element.268), channel_id=1, source_target_pairs={{0,16},{16,0},{1,17},{17,1},{2,18},{18,2},{3,19},{19,3},{4,20},{20... | collective-permute-start | bytes 3833864 | tf_op jit(solution)/shard_map/ppermute | solution.py:461
  297.2 10.3 %collective-permute-start.47 = (bf16[4,192,512]{2,1,0:T(8,128)(2,1)}, bf16[4,192,512]{2,1,0:T(8,128)(2,1)S(1)}, u32[]{:S(2)}, u32[]{:S(2)}) collective-permute-start(bf16[4,192,512]{2,1,0:T(8,128)(2,1)} %get-tuple-element.197), channel_id=1, source_target_pairs={{0,16},{16,0},{1,17},{17,1},{2,18},{18,2},{3,19},{19,3},{4,20},{20... | collective-permute-start | bytes 2359304 | tf_op jit(solution)/shard_map/ppermute | solution.py:461
  298.4 33.1 %collective-permute-start.55 = (bf16[192,512]{1,0:T(8,128)(2,1)}, bf16[192,512]{1,0:T(8,128)(2,1)}, u32[]{:S(2)}, u32[]{:S(2)}) collective-permute-start(bf16[192,512]{1,0:T(8,128)(2,1)} %add_convert_fusion.7), channel_id=1, source_target_pairs={{0,2},{1,3},{2,0},{3,1},{4,6},{5,7},{6,4},{7,5},{8,10},{9,11},{10,... | collective-permute-start | bytes 589832 | tf_op jit(solution)/shard_map/ppermute | solution.py:470
  303.2 11.4 %collective-permute-start.54 = (bf16[144,512]{1,0:T(8,128)(2,1)}, bf16[144,512]{1,0:T(8,128)(2,1)}, u32[]{:S(2)}, u32[]{:S(2)}) collective-permute-start(bf16[144,512]{1,0:T(8,128)(2,1)} %get-tuple-element.297), channel_id=1, source_target_pairs={{0,3},{1,2},{2,1},{3,0},{4,7},{5,6},{6,5},{7,4},{8,11},{9,10},{10,... | collective-permute-start | bytes 442376 | tf_op jit(solution)/shard_map/ppermute | solution.py:470
  304.5 18.8 %collective-permute-start.53 = (bf16[144,512]{1,0:T(8,128)(2,1)}, bf16[144,512]{1,0:T(8,128)(2,1)}, u32[]{:S(2)}, u32[]{:S(2)}) collective-permute-start(bf16[144,512]{1,0:T(8,128)(2,1)} %get-tuple-element.298), channel_id=1, source_target_pairs={{0,2},{1,3},{2,0},{3,1},{4,6},{5,7},{6,4},{7,5},{8,10},{9,11},{10,... | collective-permute-start | bytes 442376 | tf_op jit(solution)/shard_map/ppermute | solution.py:470
  307.5 16.6 %collective-permute-start.52 = (bf16[144,512]{1,0:T(8,128)(2,1)}, bf16[144,512]{1,0:T(8,128)(2,1)S(1)}, u32[]{:S(2)}, u32[]{:S(2)}) collective-permute-start(bf16[144,512]{1,0:T(8,128)(2,1)} %get-tuple-element.299), channel_id=1, source_target_pairs={{0,1},{1,0},{2,3},{3,2},{4,5},{5,4},{6,7},{7,6},{8,9},{9,8},{10,11... | collective-permute-start | bytes 442376 | tf_op jit(solution)/shard_map/ppermute | solution.py:470
  309.6 21.9 %collective-permute-start.51 = (f32[144,128]{1,0:T(8,128)}, f32[144,128]{1,0:T(8,128)}, u32[]{:S(2)}, u32[]{:S(2)}) collective-permute-start(f32[144,128]{1,0:T(8,128)} %reshape.365), channel_id=1, source_target_pairs={{0,16},{16,0},{1,17},{17,1},{2,18},{18,2},{3,19},{19,3},{4,20},{20... | collective-permute-start | bytes 221192 | tf_op jit(solution)/shard_map/ppermute | solution.py:461
  314.6 16.9 %collective-permute-start.50 = (bf16[192,512]{1,0:T(8,128)(2,1)}, bf16[192,512]{1,0:T(8,128)(2,1)}, u32[]{:S(2)}, u32[]{:S(2)}) collective-permute-start(bf16[192,512]{1,0:T(8,128)(2,1)} %get-tuple-element.287), channel_id=1, source_target_pairs={{0,12},{4,8},{8,4},{12,0},{1,13},{5,9},{9,5},{13,1},{2,14},{6,10},... | collective-permute-start | bytes 589832 | tf_op jit(solution)/shard_map/ppermute | solution.py:465
  334.8 13.1 %collective-permute-start.57 = (f32[144,128]{1,0:T(8,128)S(1)}, f32[144,128]{1,0:T(8,128)S(1)}, u32[]{:S(2)}, u32[]{:S(2)}) collective-permute-start(f32[144,128]{1,0:T(8,128)S(1)} %add.237), channel_id=1, source_target_pairs={{0,4},{4,0},{8,12},{12,8},{1,5},{5,1},{9,13},{13,9},{2,6},{6,2},{1... | collective-permute-start | bytes 221192 | tf_op jit(solution)/shard_map/ppermute | solution.py:465
  337.2 10.7 %collective-permute-start.62 = (bf16[144,512]{1,0:T(8,128)(2,1)S(1)}, bf16[144,512]{1,0:T(8,128)(2,1)S(1)}, u32[]{:S(2)}, u32[]{:S(2)}) collective-permute-start(bf16[144,512]{1,0:T(8,128)(2,1)S(1)} %fusion.29), channel_id=1, source_target_pairs={{0,3},{1,2},{2,1},{3,0},{4,7},{5,6},{6,5},{7,4},{8,11},{9,10},{10,... | collective-permute-start | bytes 442376 | tf_op jit(solution)/shard_map/ppermute | solution.py:470
  339.7 11.9 %collective-permute-start.61 = (bf16[144,512]{1,0:T(8,128)(2,1)S(1)}, bf16[144,512]{1,0:T(8,128)(2,1)S(1)}, u32[]{:S(2)}, u32[]{:S(2)}) collective-permute-start(bf16[144,512]{1,0:T(8,128)(2,1)S(1)} %fusion.29), channel_id=1, source_target_pairs={{0,2},{1,3},{2,0},{3,1},{4,6},{5,7},{6,4},{7,5},{8,10},{9,11},{10,... | collective-permute-start | bytes 442376 | tf_op jit(solution)/shard_map/ppermute | solution.py:470
  341.0 10.7 %collective-permute-start.60 = (bf16[144,512]{1,0:T(8,128)(2,1)S(1)}, bf16[144,512]{1,0:T(8,128)(2,1)S(1)}, u32[]{:S(2)}, u32[]{:S(2)}) collective-permute-start(bf16[144,512]{1,0:T(8,128)(2,1)S(1)} %fusion.29), channel_id=1, source_target_pairs={{0,1},{1,0},{2,3},{3,2},{4,5},{5,4},{6,7},{7,6},{8,9},{9,8},{10,11... | collective-permute-start | bytes 442376 | tf_op jit(solution)/shard_map/ppermute | solution.py:470
  343.0 10.8 %collective-permute-start.56 = (bf16[192,512]{1,0:T(8,128)(2,1)S(1)}, bf16[192,512]{1,0:T(8,128)(2,1)S(1)}, u32[]{:S(2)}, u32[]{:S(2)}) collective-permute-start(bf16[192,512]{1,0:T(8,128)(2,1)S(1)} %fusion.23), channel_id=1, source_target_pairs={{0,1},{1,0},{2,3},{3,2},{4,5},{5,4},{6,7},{7,6},{8,9},{9,8},{10,11... | collective-permute-start | bytes 589832 | tf_op jit(solution)/shard_map/ppermute | solution.py:470
  356.2 10.8 %collective-permute-start.65 = (f32[144,128]{1,0:T(8,128)S(1)}, f32[144,128]{1,0:T(8,128)S(1)}, u32[]{:S(2)}, u32[]{:S(2)}) collective-permute-start(f32[144,128]{1,0:T(8,128)S(1)} %add_add_fusion.1), channel_id=1, source_target_pairs={{0,2},{1,3},{2,0},{3,1},{4,6},{5,7},{6,4},{7,5},{8,10},{9,11},{10,... | collective-permute-start | bytes 221192 | tf_op jit(solution)/shard_map/ppermute | solution.py:470
  356.2 10.8 %collective-permute-start.64 = (f32[144,128]{1,0:T(8,128)S(1)}, f32[144,128]{1,0:T(8,128)S(1)}, u32[]{:S(2)}, u32[]{:S(2)}) collective-permute-start(f32[144,128]{1,0:T(8,128)S(1)} %add_add_fusion.1), channel_id=1, source_target_pairs={{0,1},{1,0},{2,3},{3,2},{4,5},{5,4},{6,7},{7,6},{8,9},{9,8},{10,11... | collective-permute-start | bytes 221192 | tf_op jit(solution)/shard_map/ppermute | solution.py:470
  358.3 12.1 %collective-permute-start.63 = (bf16[192,512]{1,0:T(8,128)(2,1)S(1)}, bf16[192,512]{1,0:T(8,128)(2,1)S(1)}, u32[]{:S(2)}, u32[]{:S(2)}) collective-permute-start(bf16[192,512]{1,0:T(8,128)(2,1)S(1)} %add_convert_fusion.6), channel_id=1, source_target_pairs={{0,2},{1,3},{2,0},{3,1},{4,6},{5,7},{6,4},{7,5},{8,10},{9,11},{10,... | collective-permute-start | bytes 589832 | tf_op jit(solution)/shard_map/ppermute | solution.py:470
  361.3 16.8 %collective-permute-start.68 = (bf16[576,512]{1,0:T(8,128)(2,1)S(1)}, bf16[576,512]{1,0:T(8,128)(2,1)S(1)}, u32[]{:S(2)}, u32[]{:S(2)}) collective-permute-start(bf16[576,512]{1,0:T(8,128)(2,1)S(1)} %bitcast.229), channel_id=1, source_target_pairs={{0,16},{16,0},{1,17},{17,1},{2,18},{18,2},{3,19},{19,3},{4,20},{20... | collective-permute-start | bytes 1769480 | tf_op jit(solution)/shard_map/ppermute | solution.py:461
  (67 other events, 664.4 us)
where the time goes:
time: 380 us; the launch traced here: 383 us
  Pallas kernels  159 us (42%)
  starting transfers between devices  68.6 us (18%)
  local copies, waits for them, and re-layouts  53.1 us (14%)
  other arithmetic  48.4 us (13%)
  waiting for transfers between devices  46.6 us (12%)
  matrix products  4.79 us (1%)
    pallas_call x8, Pallas kernels, run(): pl.pallas_call(kernel, grid_spec=pltpu.PrefetchScalarGridSpec(num_scalar_...  159 us
    ppermute x27, starting transfers between devices, across(): return lax.ppermute(block, 'shard', [(i, i ^ distance) for i in range(4)])  33.4 us
    ppermute x19, starting transfers between devices, along(): lax.ppermute(block, 'replica', [(i, i ^ distance) for i in range(size)])  30.7 us
    ppermute x19, waiting for transfers between devices, along(): lax.ppermute(block, 'replica', [(i, i ^ distance) for i in range(size)])  26.7 us
    convert_element_type x12, other arithmetic, add_low(): return total.astype(BF16)  15.5 us
    ppermute x27, waiting for transfers between devices, across(): return lax.ppermute(block, 'shard', [(i, i ^ distance) for i in range(4)])  14.9 us
    unnamed x102, local copies, waits for them, and re-layouts  13.7 us
  transfers between devices with their start and end apart: 69, of which 15 were waited for; matrix products, arithmetic and copies ran while one was open for 22% of the time, Pallas kernels for 30%

commit v1 on v0

--- a/solution.py
+++ b/solution.py
@@ -89,7 +89,7 @@
     return out
 
 
-def attn_load(layer, info, pieces, w_in, sems, clear=()):
+def attn_load(layer, info, pieces, w_in, sems):
     mine, other = pieces[:4], pieces[4:]
 
     def copies(source):
@@ -113,10 +113,7 @@
             for c in copies(other):
                 c.start()
 
-        for total in clear:
-            total[...] = jnp.zeros(total.shape, F32)
-        for c in copies(mine):
-            c.wait()
+    return lambda: wait_first(copies(mine))
 
 
 def mlp_copies(info, pieces, places, sems):
@@ -151,28 +148,55 @@
 ]
 
 
-def load_weights(copies, clear=()):
+def start_first(copies):
     @pl.when(pl.program_id(0) == 0)
     def _():
         for c in copies:
             c.start()
-        for total in clear:
-            total[...] = jnp.zeros(total.shape, F32)
+
+
+def wait_first(copies):
+    @pl.when(pl.program_id(0) == 0)
+    def _():
         for c in copies:
             c.wait()
 
 
+def clear_first(*totals):
+    @pl.when(pl.program_id(0) == 0)
+    def _():
+        for total in totals:
+            total[...] = jnp.zeros(total.shape, F32)
+
+
+def accumulate(total, at, value):
+    total[at] = jnp.where(pl.program_id(0) == 0, 0.0, total[at]) + value
+
+
+def pick(info, section, refs):
+    if len(refs) == 1:
+        return refs[0][0]
+    own, other = refs
+    return jnp.where(info[1] == section, own[0], other[0])
+
+
 def attn_forward_kernel(layer, info, *refs):
     pieces, refs = refs[:8], refs[8:]
-    x_ref, cut_ref, join_ref, vec_ref, bias_ref, apart_ref, *refs = refs
-    qkv_ref, p_ref, att_ref, w_in, sems, att = refs
-    attn_load(layer, info, pieces, w_in, sems)
+    count = 1 if layer else 2
+    x_refs, refs = refs[:count], refs[count:]
+    cut_ref, join_ref, vec_ref, bias_ref, apart_ref, *refs = refs
+    qkv_ref, p_ref, att_ref, *x_out, w_in, sems, att = refs
+    arrived = attn_load(layer, info, pieces, w_in, sems)
 
     @pl.when(pl.program_id(0) < info[0])
     def _():
-        xhat, _ = standard(x_ref[0].astype(F32))
+        x = pick(info, 0, x_refs)
+        for ref in x_out:
+            ref[0] = x
+        xhat, _ = standard(x.astype(F32))
         normed = (xhat * vec_ref[0:1] + vec_ref[2:3]).astype(BF16)
         normed = mm(cut_ref[...], normed).astype(BF16)
+        arrived()
         for part in range(3):
             block = mm(normed, w_in[:, 512 * part : 512 * part + 512])
             if part != 1:
@@ -202,10 +226,12 @@
     pieces, refs = refs[:8], refs[8:]
     x_ref, att_ref, vec_ref, up_bias_ref, *refs = refs
     out_ref, mid_ref, act_ref, slope_ref, w_out, w_up, w_down, sems = refs
-    load_weights(mlp_copies(info, pieces, (w_out, w_up, w_down), sems))
+    copies = mlp_copies(info, pieces, (w_out, w_up, w_down), sems)
+    start_first(copies)
 
     @pl.when(pl.program_id(0) < info[0])
     def _():
+        wait_first(copies)
         mid = x_ref[0].astype(F32) + (mm(att_ref[0], w_out[...]) + vec_ref[5:6])
         mid_ref[0] = mid
         xhat, _ = standard(mid)
@@ -241,23 +267,27 @@
     return (u - jnp.mean(u, -1, keepdims=True) - xhat * lean) * inverse
 
 
-def mlp_backward_kernel(info, *refs):
+def mlp_backward_kernel(layer, info, *refs):
     pieces, refs = refs[:8], refs[8:]
-    g_ref, att_ref, mid_ref, act_ref, slope_ref, vec_ref, *refs = refs
+    count = 2 if layer else 1
+    g_refs, refs = refs[:count], refs[count:]
+    att_ref, mid_ref, act_ref, slope_ref, vec_ref, *refs = refs
     g_mid_ref, g_att_ref, keep_ref, give_ref, vec_out, up_out, *refs = refs
     w_out, w_up, w_down, sems, d_out, d_up, d_down = refs
-    load_weights(
-        mlp_copies(info, pieces, (w_out, w_up, w_down), sems),
-        (d_out, d_up, d_down, vec_out, up_out),
-    )
+    copies = mlp_copies(info, pieces, (w_out, w_up, w_down), sems)
+    start_first(copies)
+    clear_first(vec_out, up_out)
 
     @pl.when(pl.program_id(0) < info[0])
     def _():
-        g = g_ref[0]
+        g = pick(info, 1, g_refs)
+        cols = [slice(512 * c, 512 * c + 512) for c in range(4)]
+        for c in cols:
+            accumulate(d_down, (c, slice(None)), mm_tn(act_ref[0, :, c], g))
         add_row(vec_out, 7, g.astype(F32))
         xhat, inverse = standard(mid_ref[0])
         normed_two = (xhat * vec_ref[1:2] + vec_ref[6:7]).astype(BF16)
-        cols = [slice(512 * c, 512 * c + 512) for c in range(4)]
+        wait_first(copies)
         g_hidden = []
         for c in cols:
             part = (mm_nt(g, w_down[c, :]) * slope_ref[0, :, c].astype(F32)).astype(BF16)
@@ -265,13 +295,12 @@
             g_hidden.append(part)
         g_normed = sum(mm_nt(part, w_up[:, c]) for part, c in zip(g_hidden, cols))
         for part, c in zip(g_hidden, cols):
-            d_down[:, c] += mm_tn(g, act_ref[0, :, c])
-            d_up[:, c] += mm_tn(normed_two, part)
+            accumulate(d_up, (slice(None), c), mm_tn(normed_two, part))
         g_mid = g.astype(F32) + norm_back(vec_out, (1, 6), g_normed, xhat, inverse, vec_ref[1:2])
         g_mid_ref[0] = g_mid
         g_update = g_mid.astype(BF16)
         add_row(vec_out, 5, g_update.astype(F32))
-        d_out[...] += mm_tn(att_ref[0], g_update)
+        accumulate(d_out, Ellipsis, mm_tn(att_ref[0], g_update))
         g_att_ref[0] = mm_nt(g_update, w_out[...]).astype(BF16)
 
     @pl.when(pl.program_id(0) == pl.num_programs(0) - 1)
@@ -285,7 +314,7 @@
                         rows, 512 * c : 512 * c + 512
                     ].astype(BF16)
                 deep = pl.ds(pl.multiple_of(512 * shard + 256 * half, 256), 256)
-                out_ref[at, 256:512, :] = d_down[:, deep].T.astype(BF16)
+                out_ref[at, 256:512, :] = d_down[deep, :].astype(BF16)
                 out_ref[at, 512:576, :] = d_out[rows, :].astype(BF16)
 
 
@@ -293,8 +322,9 @@
     pieces, refs = refs[:8], refs[8:]
     g_mid_ref, g_att_ref, x_ref, qkv_ref, p_ref, cut_ref, join_ref, vec_ref, *refs = refs
     gx_ref, keep_ref, give_ref, vec_out, table_out, *refs = refs
-    w_in, sems, d_in, g_att, gqkv = refs
-    attn_load(layer, info, pieces, w_in, sems, (d_in, vec_out, table_out))
+    w_in, sems, d_in, g_att, gqkv, table_sum = refs
+    arrived = attn_load(layer, info, pieces, w_in, sems)
+    clear_first(vec_out, table_sum)
 
     @pl.when(pl.program_id(0) < info[0])
     def _():
@@ -319,14 +349,15 @@
             gqkv[rows, lanes(1)] = (g_k[n] * 32**-0.5).astype(BF16)
             gqkv[rows, lanes(2)] = g_v[n].astype(BF16)
         for h in range(GROUPS):
-            table_out[h] += sum(g_s[n].astype(F32) for n in at if BLOCKS[n][2] == h)
+            table_sum[h] += sum(g_s[n].astype(F32) for n in at if BLOCKS[n][2] == h)
+        arrived()
         xhat, inverse = standard(x_ref[0].astype(F32))
         normed = (xhat * vec_ref[0:1] + vec_ref[2:3]).astype(BF16)
         g_normed = None
         for part in range(3):
             cols = slice(512 * part, 512 * part + 512)
             block = mm(join_ref[...], gqkv[:, cols]).astype(BF16)
-            d_in[:, cols] += mm_tn(normed, block)
+            accumulate(d_in, (slice(None), cols), mm_tn(normed, block))
             if part != 1:
                 add_row(vec_out, 3 if part == 0 else 4, block.astype(F32))
             term = mm_nt(block, w_in[:, cols])
@@ -336,6 +367,9 @@
 
     @pl.when(pl.program_id(0) == pl.num_programs(0) - 1)
     def _():
+        for h in range(HEADS):
+            lanes = slice(h % QUAD * SLOT, h % QUAD * SLOT + SLOT)
+            table_out[h] = table_sum[h // QUAD, :, lanes]
         for out_ref, half in ((keep_ref, info[1]), (give_ref, 1 - info[1])):
             for shard in range(4):
                 at = jnp.bitwise_xor(info[2], shard)
@@ -372,27 +406,37 @@
 ]
 
 
-def run(kernel, info, pieces, by_image, shared, outs, shared_outs, scratch, micros):
-    count = by_image[0].shape[0]
+def by_slot(shape):
+    def place(i, info):
+        return (info[3 + jnp.maximum(jnp.minimum(i, info[0] - 1), 0)],) + (0,) * len(shape)
+
+    return pl.BlockSpec((1,) + shape, place)
+
+
+def run(kernel, info, pieces, slotted, by_image, shared, outs, shared_outs, scratch, micros, slot_outs=()):
+    count = info.shape[0] - 3
     return pl.pallas_call(
         kernel,
         grid_spec=pltpu.PrefetchScalarGridSpec(
             num_scalar_prefetch=1,
             grid=(count,),
             in_specs=[pl.BlockSpec(memory_space=pl.ANY)] * len(pieces)
+            + [by_slot(a.shape[1:]) for a in slotted]
             + [each(a.shape[1:]) for a in by_image]
             + [whole(a.shape) for a in shared],
-            out_specs=[each(shape) for shape, _ in outs]
+            out_specs=[by_slot(shape[1:]) for shape, _ in slot_outs]
+            + [each(shape) for shape, _ in outs]
             + [whole(shape) for shape, _ in shared_outs],
             scratch_shapes=scratch,
         ),
-        out_shape=[jax.ShapeDtypeStruct((count,) + shape, kind) for shape, kind in outs]
+        out_shape=[jax.ShapeDtypeStruct(shape, kind) for shape, kind in slot_outs]
+        + [jax.ShapeDtypeStruct((count,) + shape, kind) for shape, kind in outs]
         + [jax.ShapeDtypeStruct(shape, kind) for shape, kind in shared_outs],
         compiler_params=pltpu.CompilerParams(vmem_limit_bytes=56 * 1024 * 1024),
         cost_estimate=pl.CostEstimate(
             flops=int(micros * 1e9), bytes_accessed=int(micros * 1e6), transcendentals=0
         ),
-    )(info, *pieces, *by_image, *shared)
+    )(info, *pieces, *slotted, *by_image, *shared)
 
 
 def attn_forward(layer, info, pieces, x, cut, join, vec, bias, apart):
@@ -400,60 +444,67 @@
         functools.partial(attn_forward_kernel, layer),
         info,
         pieces,
-        [x],
+        [] if layer else x,
+        [x] if layer else [],
         [cut, join, vec, bias, apart],
-        [QKV, PROB, X],
+        [QKV, PROB, X] + ([] if layer else [X]),
         [],
         ATTN_WEIGHTS + [pltpu.VMEM((ROWS, 512), BF16)],
         20,
     )
 
 
-def mlp_forward(info, pieces, x, att, vec, up_bias):
+def mlp_forward(info, pieces, x, att, vec, up_bias, slots=None):
     return run(
         mlp_forward_kernel,
         info,
         pieces,
+        [],
         [x, att],
         [vec, up_bias],
-        [X, MID, WIDE_X, WIDE_X],
+        ([] if slots else [X]) + [MID, WIDE_X, WIDE_X],
         [],
         MLP_WEIGHTS,
         20,
-    )
-
-
-def mlp_backward(info, pieces, g, att, mid, act, slope, vec):
+        [((slots,) + X[0], BF16)] if slots else [],
+    )
+
+
+def mlp_backward(layer, info, pieces, g, att, mid, act, slope, vec):
     return run(
-        mlp_backward_kernel,
+        functools.partial(mlp_backward_kernel, layer),
         info,
         pieces,
-        [g, att, mid, act, slope],
+        g if layer else [],
+        ([] if layer else [g]) + [att, mid, act, slope],
         [vec],
         [MID, X],
         [((4, 576, 512), BF16)] * 2 + [VEC, ((1, 2048), F32)],
         MLP_WEIGHTS
-        + [pltpu.VMEM((512, 512), F32), pltpu.VMEM((512, 2048), F32), pltpu.VMEM((512, 2048), F32)],
+        + [pltpu.VMEM((512, 512), F32), pltpu.VMEM((512, 2048), F32), pltpu.VMEM((2048, 512), F32)],
         30,
     )
 
 
-def attn_backward(layer, info, pieces, g_mid, g_att, x, qkv, p, cut, join, vec):
+def attn_backward(layer, info, pieces, g_mid, g_att, x, qkv, p, cut, join, vec, slots=None):
     return run(
         functools.partial(attn_backward_kernel, layer),
         info,
         pieces,
+        [],
         [g_mid, g_att, x, qkv, p],
         [cut, join, vec],
-        [X],
-        [((4, 192, 512), BF16)] * 2 + [VEC, ((GROUPS, SLOT, WIDE), F32)],
+        [] if slots else [X],
+        [((4, 192, 512), BF16)] * 2 + [VEC, ((HEADS, SLOT, SLOT), F32)],
         ATTN_WEIGHTS
         + [
             pltpu.VMEM((512, 1536), F32),
             pltpu.VMEM((ROWS, 512), BF16),
             pltpu.VMEM((ROWS, 1536), BF16),
+            pltpu.VMEM((GROUPS, SLOT, WIDE), F32),
         ],
         30,
+        [((slots,) + X[0], BF16)] if slots else [],
     )
 
 
@@ -498,14 +549,14 @@
 
 def reduce_steps(keep, give, quick):
     (got,) = yield [swap(give)]
-    total = add_low(keep, got)
+    total = [add_low(keep[d], got[d]) for d in range(4)]
     got = yield [across(total[d], d) for d in (1, 2, 3)]
     owned = add_low(total[0], *got)
     size = lax.axis_size("replica")
     if size != 4:
         return lax.psum(owned, "replica")
     if quick:
-        for d in (1, 2):
+        for d in quick:
             (got,) = yield [along(owned, d)]
             owned = add_low(owned, got)
         return owned
@@ -580,14 +631,12 @@
     owner = jnp.bitwise_and(rank, 1)
     place = jnp.right_shift(rank, 1)
 
-    def slots_of(whose):
-        hit = present & (owner == whose)
-        hit = hit[None] & (place[None] == jnp.arange(share)[:, None])
-        return jnp.sum(jnp.where(hit, jnp.arange(slots)[None], 0), 1)
-
+    hit = present & (owner == core)
+    hit = hit[None] & (place[None] == jnp.arange(share)[:, None])
+    own_slots = jnp.sum(jnp.where(hit, jnp.arange(slots)[None], 0), 1)
     total_images = jnp.sum(present.astype(jnp.int32))
     own_count = jnp.right_shift(total_images + 1 - core, 1)
-    info = jnp.stack([own_count, core, me]).astype(jnp.int32)
+    info = jnp.concatenate([jnp.stack([own_count, core, me]), own_slots]).astype(jnp.int32)
 
     flat = jnp.concatenate(
         [
@@ -624,10 +673,7 @@
 
     framed = boundary.reshape(slots, TOKENS, 512)
     framed = jnp.pad(framed, ((0, 0), (0, FRAME - TOKENS), (0, 0)))
-    kept = framed[slots_of(core)]
-    other = swap(framed[slots_of(1 - core)])
-    images = jnp.where(first, kept, other)
-    cotangents = jnp.where(first, other, kept)
+    framed = [framed, swap(framed)]
 
     small = by_distance(jnp.stack([flat] + [across(flat, d) for d in (1, 2, 3)]), me)
     small_other = swap(small)
@@ -654,28 +700,32 @@
     apart = apart.astype(F32)
 
     cut = [jnp.asarray(window_place(shift), BF16) for shift in (0, SHIFT)]
-    x, saved = images, []
+    x, saved = framed, []
     for layer in range(2):
         vec = vecs[layer]
-        qkv, p, att = attn_forward(
+        qkv, p, att, *images = attn_forward(
             layer, info, attn_pieces, x, cut[layer], cut[layer].T, vec, bias[layer], apart
         )
         if layer == 0:
+            (x,) = images
             att, mlp_mine, mlp_second = tie(att, mlp_mine, mlp_own[1])
             mlp_pieces = [with_other(mlp_mine)]
             mlp_mine = gather_direct(mlp_second)
-        out, mid, act, slope = mlp_forward(info, mlp_pieces[layer], x, att, vec, lifts[layer])
+        out, mid, act, slope = mlp_forward(
+            info, mlp_pieces[layer], x, att, vec, lifts[layer], slots if layer else None
+        )
         if layer == 0:
             out, mlp_mine = tie(out, mlp_mine)
             mlp_pieces.append(with_other(mlp_mine))
         saved.append((x, qkv, p, att, mid, act, slope))
         x = out
-    output, g = x, cotangents
+    output = x
+    output_other = lax.ppermute(output, "section", [(0, 1)])
     small_sums = [None, None]
 
     def backward_mlp(layer, g):
         x, qkv, p, att, mid, act, slope = saved[layer]
-        return mlp_backward(info, mlp_pieces[layer], g, att, mid, act, slope, vecs[layer])
+        return mlp_backward(layer, info, mlp_pieces[layer], g, att, mid, act, slope, vecs[layer])
 
     def backward_attn(layer, g_mid, g_att):
         x, qkv, p, *_ = saved[layer]
@@ -691,50 +741,54 @@
             cut[layer],
             cut[layer].T,
             vecs[layer],
+            None if layer else slots,
         )
 
     def small_of(vec, up, table):
-        table = table.reshape(GROUPS, SLOT, QUAD, SLOT).transpose(0, 2, 1, 3)
         table = table.reshape(HEADS, SLOT * SLOT)
         table = lax.dot_general(
             table, onehot.astype(F32), (((1,), (1,)), ((), ())), precision=lax.Precision.HIGHEST
         )
         return jnp.concatenate([vec.reshape(-1), up.reshape(-1), table.reshape(-1)])
 
-    g_mid, g_att, *sums, mlp_vec, up_sums = backward_mlp(1, g)
-    second_mlp = Flow(reduce_steps(*sums, False))
+    g_mid, g_att, *sums, mlp_vec, up_sums = backward_mlp(1, framed)
+    second_mlp = Flow(reduce_steps(*sums, (2, 1)))
     g_mid, g_att = boundary_of((g_mid, g_att), [second_mlp])
     g, *sums, attn_vec, table = backward_attn(1, g_mid, g_att)
     second_small = (mlp_vec + attn_vec, up_sums, table)
     g, sums = boundary_of((g, sums), [second_mlp])
-    second_attn = Flow(reduce_steps(*sums, True))
+    second_attn = Flow(reduce_steps(*sums, (1, 2)))
     g = boundary_of(g, [second_attn])
     g_mid, g_att, *sums, mlp_vec, up_sums = backward_mlp(0, g)
     second_small = small_of(*second_small)
     g_mid, g_att, sums, second_small = boundary_of(
         (g_mid, g_att, sums, second_small), [second_mlp, second_attn]
     )
-    first_mlp = Flow(reduce_steps(*sums, False))
+    first_mlp = Flow(reduce_steps(*sums, (2, 1)))
     g_mid, g_att = boundary_of((g_mid, g_att), [first_mlp])
     g, *sums, attn_vec, table = backward_attn(0, g_mid, g_att)
-    first_attn = Flow(reduce_steps(*sums, True))
-    g = boundary_of(g, [second_mlp, second_attn, first_mlp])
-    hold = jnp.where(first, g, output)
-    back = swap(jnp.where(first, output, g))
+    g, sums = boundary_of((g, sums), [second_mlp, second_attn, first_mlp])
+    first_attn = Flow(reduce_steps(*sums, (1, 2)))
+    g, mlp_vec, up_sums, attn_vec, table = boundary_of(
+        (g, mlp_vec, up_sums, attn_vec, table), [first_attn]
+    )
     small = jnp.stack([small_of(mlp_vec + attn_vec, up_sums, table), second_small])
     width = small.shape[1]
     small = jnp.pad(small, ((0, 0), (0, -width % 1024))).reshape(-1, 128)
-    back, small = boundary_of((back, small), [first_attn])
+    g, small = boundary_of((g, small), [first_attn, first_mlp, second_attn])
+    back = lax.ppermute(g, "section", [(1, 0)])
     small_flow = Flow(sum_steps(small))
 
-    every = jnp.concatenate([hold, back], 0)
-    source = jnp.clip(jnp.where(owner == core, 0, share) + place, 0, 2 * share - 1)
-    chosen = every[source][:, :TOKENS]
-    chosen = jnp.where(present[:, None, None], chosen, jnp.zeros((), BF16))
+    mine = owner == core
+    pair = (jnp.where(first, g, output), jnp.where(first, back, output_other))
+    chosen = jnp.where(mine[:, None, None], *pair)
+    chosen = jnp.where(present[:, None, None], chosen, jnp.zeros((), BF16))[:, :TOKENS]
     results = chosen.reshape(1, mb_count, per_device, SIDE, SIDE, 512)
-    results = boundary_of(results, [first_attn, small_flow, first_mlp, second_attn])
-    flows = [first_attn, small_flow, second_attn, first_mlp, second_mlp]
-    while any(flow.total is None for flow in flows[1:]):
+    boundary_of((), [first_attn, small_flow])
+    results = boundary_of(results, [small_flow])
+    boundary_of((), [first_attn, first_mlp, small_flow])
+    flows = [first_attn, small_flow, first_mlp, second_attn, second_mlp]
+    while any(flow.total is None for flow in flows):
         boundary_of((), flows)
 
     def exchanged(one, two):
@@ -742,15 +796,15 @@
         back = swap(jnp.where(first, two, one))
         return jnp.stack([jnp.where(first, hold, back), jnp.where(first, back, hold)])
 
-    mlp = exchanged(first_mlp.total, second_mlp.total)
-    while first_attn.total is None:
-        (mlp,) = boundary_of((mlp,), [first_attn])
-    mlp = mlp.astype(F32)
-    attn = exchanged(first_attn.total, second_attn.total).astype(F32)
-    grad_in = attn.reshape(2, 3, 64, 512).transpose(0, 2, 1, 3).reshape(128, 1536)
-    grad_up = mlp[:, 0:256].reshape(2, 4, 64, 512).transpose(0, 2, 1, 3).reshape(128, 2048)
-    grad_down = mlp[:, 256:512].reshape(512, 512)
-    grad_out = mlp[:, 512:576].reshape(128, 512)
+    one, two = [
+        jnp.concatenate([attn.total, mlp.total], 0)
+        for attn, mlp in ((first_attn, first_mlp), (second_attn, second_mlp))
+    ]
+    both = exchanged(one, two).astype(F32)
+    grad_in = both[:, 0:192].reshape(2, 3, 64, 512).transpose(0, 2, 1, 3).reshape(128, 1536)
+    grad_up = both[:, 192:448].reshape(2, 4, 64, 512).transpose(0, 2, 1, 3).reshape(128, 2048)
+    grad_down = both[:, 448:704].reshape(512, 512)
+    grad_out = both[:, 704:768].reshape(128, 512)
 
     bundle = small_flow.total.reshape(2, -1)[:, :width]
     bundle = lax.dynamic_index_in_dim(bundle, core, 0, keepdims=False)

time: 380 us -> 369 us (0.971); the launches traced: 383 us -> 365 us
  waiting for transfers between devices: 46.6 us -> 64.4 us
  other arithmetic: 48.4 us -> 35.2 us
  starting transfers between devices: 68.6 us -> 55.4 us
  local copies, waits for them, and re-layouts: 53.1 us -> 41.4 us
    ppermute x19 -> x11, starting transfers between devices: 30.7 us -> 14.2 us  [along(): lax.ppermute(block, 'replica', [(i, i ^ distance) for i in range(size)])]
    select_n x8 -> x1, other arithmetic: 13.6 us -> 1.87 us  [body(): jnp.where(present[:, None, None], chosen, jnp.zeros((), BF16))[:, :TOKENS]]
    gather x4 -> x0, local copies, waits for them, and re-layouts: 10.1 us -> none  [the longest x2 6.02 us: body(): other = swap(framed[slots_of(1 - core)])]
    ppermute x27, waiting for transfers between devices: 14.9 us -> 24.9 us  [across(): return lax.ppermute(block, 'shard', [(i, i ^ distance) for i in range(4)])]
    convert_element_type x12 -> x16, other arithmetic: 15.5 us -> 21.7 us  [add_low(): return total.astype(BF16)]
    squeeze x6 -> x0, local copies, waits for them, and re-layouts: 4.2 us -> none  [the longest x4 3.39 us: reduce_steps(): got = (yield [across(total[d], d) for d in (1, 2, 3)])]
    ppermute x23 -> x21, waiting for transfers between devices: 4.96 us -> 8.94 us  [swap(): return lax.ppermute(block, 'section', [(0, 1), (1, 0)])]
    ppermute x19 -> x11, waiting for transfers between devices: 26.7 us -> 30.5 us  [along(): lax.ppermute(block, 'replica', [(i, i ^ distance) for i in range(size)])]
  transfers between devices with their start and end apart: 69 -> 61, of which waited for: 15 -> 16; matrix products, arithmetic and copies ran while one was open for 22% -> 16% of each run, Pallas kernels for 30% -> 32%
where the time goes in v1:
time: 369 us; the launch traced here: 365 us
  Pallas kernels  161 us (44%)
  waiting for transfers between devices  64.4 us (17%)
  starting transfers between devices  55.4 us (15%)
  local copies, waits for them, and re-layouts  41.4 us (11%)
  other arithmetic  35.2 us (10%)
  matrix products  5.16 us (1%)
    pallas_call x8, Pallas kernels, run(): pl.pallas_call(kernel, grid_spec=pltpu.PrefetchScalarGridSpec(num_scalar_...  161 us
    ppermute x27, starting transfers between devices, across(): return lax.ppermute(block, 'shard', [(i, i ^ distance) for i in range(4)])  32.7 us
    ppermute x11, waiting for transfers between devices, along(): lax.ppermute(block, 'replica', [(i, i ^ distance) for i in range(size)])  30.5 us
    ppermute x27, waiting for transfers between devices, across(): return lax.ppermute(block, 'shard', [(i, i ^ distance) for i in range(4)])  24.9 us
    convert_element_type x16, other arithmetic, add_low(): return total.astype(BF16)  21.7 us
    unnamed x136, local copies, waits for them, and re-layouts  14.5 us
    ppermute x11, starting transfers between devices, along(): lax.ppermute(block, 'replica', [(i, i ^ distance) for i in range(size)])  14.2 us
    ppermute x21, waiting for transfers between devices, swap(): return lax.ppermute(block, 'section', [(0, 1), (1, 0)])  8.94 us
  transfers between devices with their start and end apart: 61, of which 16 were waited for; matrix products, arithmetic and copies ran while one was open for 16% of the time, Pallas kernels for 32%

profile of v1, /device:TPU:0, one launch (start us, length us, event | category | flops | bytes accessed | tf_op | source)
XLA Modules:
  0.0 364.8 jit_solution(6037275616617705728)
XLA Ops:
  3.9 3.0 collective-permute-start.10
  8.5 2.9 collective-permute-start.2
  17.1 2.3 copy.65
  19.5 2.8 reshape.315
  22.2 3.4 pad.21.refs_8_
  27.1 3.1 collective-permute-done.11
  37.8 2.3 collective-permute-start.15
  42.1 14.6 %shard_map.205 = (bf16[6,256,1536]{2,1,0:T(8,128)(2,1)}, bf16[6,4,4,64,256]{4,3,2,1,0:T(8,128)(2,1)}, bf16[6,208,512]{2,1,0:T(8,128)(2,1)}, bf16[6,208,512]{2,1,0:T(8,128)(2,1)}) custom-call(s32[9]{0:T(128)} %pad_add_fusion.info, bf16[384,512]{1,0:T(8,128)(2,1)} %bitcast.7.refs_0_, bf16[384,512]{1,0:T(8,128)(2,1)} %collective-permute-done.refs_1_, ...), custom_call_target="tpu_custom_call" | custom-call | flops 20000000000 | bytes 20000000 | tf_op jit(solution)/shard_map/pallas_call | solution.py:418
  56.7 9.9 %collective-permute-done.14.refs_2_ = bf16[576,512]{1,0:T(8,128)(2,1)S(1)} collective-permute-done((bf16[576,512]{1,0:T(8,128)(2,1)S(1)}, bf16[576,512]{1,0:T(8,128)(2,1)S(1)}, u32[]{:S(2)}, u32[]{:S(2)}) %collective-permute-start.14) | collective-permute-done | bytes 589856 | tf_op jit(solution)/shard_map/ppermute | solution.py:516
  69.0 1.7 collective-permute-start.22
  73.5 19.2 %shard_map.206 = (bf16[6,208,512]{2,1,0:T(8,128)(2,1)}, f32[6,208,512]{2,1,0:T(8,128)}, bf16[6,208,2048]{2,1,0:T(8,128)(2,1)}, bf16[6,208,2048]{2,1,0:T(8,128)(2,1)}) custom-call(s32[9]{0:T(128)} %pad_add_fusion.info, bf16[576,512]{1,0:T(8,128)(2,1)} %copy-done.18, bf16[576,512]{1,0:T(8,128)(2,1)} %copy-done.47, bf16[576,512]{1,0:T(8,128)(2,1)} %copy-done.46, ...), custom_call_target="tpu_custom_call" | custom-call | flops 20000000000 | bytes 20000000 | tf_op jit(solution)/shard_map/pallas_call | solution.py:418
  92.7 5.1 %collective-permute-done.21.refs_2_ = bf16[576,512]{1,0:T(8,128)(2,1)S(1)} collective-permute-done((bf16[576,512]{1,0:T(8,128)(2,1)S(1)}, bf16[576,512]{1,0:T(8,128)(2,1)S(1)}, u32[]{:S(2)}, u32[]{:S(2)}) %collective-permute-start.21) | collective-permute-done | bytes 589856 | tf_op jit(solution)/shard_map/ppermute | solution.py:516
  98.9 14.4 %shard_map.207 = (bf16[6,256,1536]{2,1,0:T(8,128)(2,1)}, bf16[6,4,4,64,256]{4,3,2,1,0:T(8,128)(2,1)}, bf16[6,208,512]{2,1,0:T(8,128)(2,1)}) custom-call(s32[9]{0:T(128)} %pad_add_fusion.info, bf16[384,512]{1,0:T(8,128)(2,1)} %bitcast.7.refs_0_, bf16[384,512]{1,0:T(8,128)(2,1)} %collective-permute-done.refs_1_, ...), custom_call_target="tpu_custom_call" | custom-call | flops 20000000000 | bytes 20000000 | tf_op jit(solution)/shard_map/pallas_call | solution.py:418
  114.8 19.4 %shard_map.208 = (bf16[12,208,512]{2,1,0:T(8,128)(2,1)}, f32[6,208,512]{2,1,0:T(8,128)}, bf16[6,208,2048]{2,1,0:T(8,128)(2,1)}, bf16[6,208,2048]{2,1,0:T(8,128)(2,1)}) custom-call(s32[9]{0:T(128)} %pad_add_fusion.info, bf16[576,512]{1,0:T(8,128)(2,1)} %copy-done.19, bf16[576,512]{1,0:T(8,128)(2,1)} %copy-done.54, bf16[576,512]{1,0:T(8,128)(2,1)} %copy-done.53, ...), custom_call_target="tpu_custom_call" | custom-call | flops 20000000000 | bytes 20000000 | tf_op jit(solution)/shard_map/pallas_call | solution.py:418
  134.2 25.6 %shard_map.209 = (f32[6,208,512]{2,1,0:T(8,128)}, bf16[6,208,512]{2,1,0:T(8,128)(2,1)}, bf16[4,576,512]{2,1,0:T(8,128)(2,1)}, bf16[4,576,512]{2,1,0:T(8,128)(2,1)}, f32[8,512]{1,0:T(8,128)}, /*index=5*/f32[1,2048]{1,0:T(1,128)}) custom-call(s32[9]{0:T(128)} %pad_add_fusion.info, bf16[576,512]{1,0:T(8,128)(2,1)} %copy-done.19, bf16[576,512]{1,0:T(8,128)(2,1)} %copy-done.54, ...), custom_call_target="tpu_custom_call" | custom-call | flops 30000001024 | bytes 30000000 | tf_op jit(solution)/shard_map/pallas_call | solution.py:418
  160.0 4.6 %collective-permute-done.27 = bf16[4,576,512]{2,1,0:T(8,128)(2,1)S(1)} collective-permute-done((bf16[4,576,512]{2,1,0:T(8,128)(2,1)}, bf16[4,576,512]{2,1,0:T(8,128)(2,1)S(1)}, u32[]{:S(2)}, u32[]{:S(2)}) %collective-permute-start.27) | collective-permute-done | bytes 2359328 | tf_op jit(solution)/shard_map/ppermute | solution.py:512
  164.6 1.9 fusion.24
  166.5 1.8 collective-permute-start.30
  170.0 21.1 %shard_map.210 = (bf16[6,208,512]{2,1,0:T(8,128)(2,1)}, bf16[4,192,512]{2,1,0:T(8,128)(2,1)}, bf16[4,192,512]{2,1,0:T(8,128)(2,1)}, f32[8,512]{1,0:T(8,128)}, f32[16,64,64]{2,1,0:T(8,128)}) custom-call(s32[9]{0:T(128)} %pad_add_fusion.info, bf16[384,512]{1,0:T(8,128)(2,1)} %bitcast.7.refs_0_, bf16[384,512]{1,0:T(8,128)(2,1)} %collective-permute-done.refs_1_, ...), custom_call_target="tpu_custom_call" | custom-call | flops 30000001024 | bytes 30000000 | tf_op jit(solution)/shard_map/pallas_call | solution.py:418
  191.1 4.4 %collective-permute-done.29 = bf16[576,512]{1,0:T(8,128)(2,1)} collective-permute-done((bf16[576,512]{1,0:T(8,128)(2,1)S(1)}, bf16[576,512]{1,0:T(8,128)(2,1)}, u32[]{:S(2)}, u32[]{:S(2)}) %collective-permute-start.29) | collective-permute-done | bytes 589856 | tf_op jit(solution)/shard_map/ppermute | solution.py:516
  199.1 2.1 fusion.21
  201.2 2.7 collective-permute-start.32
  205.1 1.7 collective-permute-start.35
  208.7 25.4 %shard_map.211 = (f32[6,208,512]{2,1,0:T(8,128)}, bf16[6,208,512]{2,1,0:T(8,128)(2,1)}, bf16[4,576,512]{2,1,0:T(8,128)(2,1)}, bf16[4,576,512]{2,1,0:T(8,128)(2,1)}, f32[8,512]{1,0:T(8,128)}, /*index=5*/f32[1,2048]{1,0:T(1,128)}) custom-call(s32[9]{0:T(128)} %pad_add_fusion.info, bf16[576,512]{1,0:T(8,128)(2,1)} %copy-done.18, bf16[576,512]{1,0:T(8,128)(2,1)} %copy-done.47, ...), custom_call_target="tpu_custom_call" | custom-call | flops 30000001024 | bytes 30000000 | tf_op jit(solution)/shard_map/pallas_call | solution.py:418
  235.4 1.6 collective-permute-start.38
  239.0 1.5 fusion.28
  240.4 1.7 collective-permute-start.41
  243.9 21.0 %shard_map.212 = (bf16[12,208,512]{2,1,0:T(8,128)(2,1)}, bf16[4,192,512]{2,1,0:T(8,128)(2,1)}, bf16[4,192,512]{2,1,0:T(8,128)(2,1)}, f32[8,512]{1,0:T(8,128)}, f32[16,64,64]{2,1,0:T(8,128)}) custom-call(s32[9]{0:T(128)} %pad_add_fusion.info, bf16[384,512]{1,0:T(8,128)(2,1)} %bitcast.7.refs_0_, bf16[384,512]{1,0:T(8,128)(2,1)} %collective-permute-done.refs_1_, ...), custom_call_target="tpu_custom_call" | custom-call | flops 30000001024 | bytes 30000000 | tf_op jit(solution)/shard_map/pallas_call | solution.py:418
  265.0 4.6 %collective-permute-done.40 = bf16[576,512]{1,0:T(8,128)(2,1)S(1)} collective-permute-done((bf16[576,512]{1,0:T(8,128)(2,1)}, bf16[576,512]{1,0:T(8,128)(2,1)S(1)}, u32[]{:S(2)}, u32[]{:S(2)}) %collective-permute-start.40) | collective-permute-done | bytes 589856 | tf_op jit(solution)/shard_map/ppermute | solution.py:516
  271.6 1.9 fusion.18
  273.5 2.7 collective-permute-start.46
  278.0 2.5 fusion.3
  280.6 2.2 fusion.42
  282.9 1.6 collective-permute-start.45
  286.5 10.4 %collective-permute-done.47 = bf16[192,512]{1,0:T(8,128)(2,1)} collective-permute-done((bf16[192,512]{1,0:T(8,128)(2,1)S(1)}, bf16[192,512]{1,0:T(8,128)(2,1)}, u32[]{:S(2)}, u32[]{:S(2)}) %collective-permute-start.47) | collective-permute-done | bytes 196640 | tf_op jit(solution)/shard_map/ppermute | solution.py:521
  298.4 10.2 %collective-permute-done.46 = bf16[576,512]{1,0:T(8,128)(2,1)} collective-permute-done((bf16[576,512]{1,0:T(8,128)(2,1)S(1)}, bf16[576,512]{1,0:T(8,128)(2,1)}, u32[]{:S(2)}, u32[]{:S(2)}) %collective-permute-start.46) | collective-permute-done | bytes 589856 | tf_op jit(solution)/shard_map/ppermute | solution.py:521
  314.1 2.2 add_convert_fusion.2
  316.3 1.9 collective-permute-start.56
  318.2 3.7 %collective-permute-done.50 = bf16[192,512]{1,0:T(8,128)(2,1)S(1)} collective-permute-done((bf16[192,512]{1,0:T(8,128)(2,1)S(1)}, bf16[192,512]{1,0:T(8,128)(2,1)S(1)}, u32[]{:S(2)}, u32[]{:S(2)}) %collective-permute-start.50) | collective-permute-done | bytes 196640 | tf_op jit(solution)/shard_map/ppermute | solution.py:521
  321.9 1.7 collective-permute-start.54
  326.2 1.9 fusion.6
  328.1 2.7 reshape.332
  331.8 2.2 collective-permute-start.59
  337.3 3.0 collective-permute-done.55
  340.4 3.2 collective-permute-done.58
  348.0 3.7 %copy.77 = bf16[1,4,3,14,14,512]{5,1,4,3,2,0:T(4,128)(2,1)} copy(bf16[1,4,3,14,14,512]{5,4,3,2,1,0:T(8,128)(2,1)S(1)} %reshape.332) | data formatting | bytes 4816896
  355.5 1.7 select_bitcast_fusion.1
  360.9 1.7 broadcast_in_dim_reshape.16
  (327 shorter events, 75.3 us)
Async XLA Ops:
  3.9 21.7 %collective-permute-start.10 = (bf16[24,128]{1,0:T(8,128)(2,1)S(1)}, bf16[24,128]{1,0:T(8,128)(2,1)S(1)}, u32[]{:S(2)}, u32[]{:S(2)}) collective-permute-start(bf16[24,128]{1,0:T(8,128)(2,1)S(1)} %fusion.55), channel_id=1, source_target_pairs={{0,8},{4,12},{8,0},{12,4},{1,9},{5,13},{9,1},{13,5},{2,10},{6,14},... | collective-permute-start | bytes 18440 | tf_op jit(solution)/shard_map/ppermute | solution.py:516
  7.0 18.8 %collective-permute-start.9 = (bf16[24,128]{1,0:T(8,128)(2,1)S(1)}, bf16[24,128]{1,0:T(8,128)(2,1)S(1)}, u32[]{:S(2)}, u32[]{:S(2)}) collective-permute-start(bf16[24,128]{1,0:T(8,128)(2,1)S(1)} %fusion.55), channel_id=1, source_target_pairs={{0,12},{4,8},{8,4},{12,0},{1,13},{5,9},{9,5},{13,1},{2,14},{6,10},... | collective-permute-start | bytes 18440 | tf_op jit(solution)/shard_map/ppermute | solution.py:516
  8.4 17.3 %collective-permute-start.8 = (bf16[24,128]{1,0:T(8,128)(2,1)S(1)}, bf16[24,128]{1,0:T(8,128)(2,1)S(1)}, u32[]{:S(2)}, u32[]{:S(2)}) collective-permute-start(bf16[24,128]{1,0:T(8,128)(2,1)S(1)} %fusion.55), channel_id=1, source_target_pairs={{0,4},{4,0},{8,12},{12,8},{1,5},{5,1},{9,13},{13,9},{2,6},{6,2},{1... | collective-permute-start | bytes 18440 | tf_op jit(solution)/shard_map/ppermute | solution.py:516
  8.5 25.8 %collective-permute-start.2 = (bf16[384,512]{1,0:T(8,128)(2,1)}, bf16[384,512]{1,0:T(8,128)(2,1)}, u32[]{:S(2)}, u32[]{:S(2)}) collective-permute-start(bf16[384,512]{1,0:T(8,128)(2,1)} %bitcast.7.refs_0_), channel_id=1, source_target_pairs={{0,12},{4,8},{8,4},{12,0},{1,13},{5,9},{9,5},{13,1},{2,14},{6,10},... | collective-permute-start | bytes 1179656 | tf_op jit(solution)/shard_map/ppermute | solution.py:516
  11.4 23.0 %collective-permute-start.1 = (bf16[384,512]{1,0:T(8,128)(2,1)}, bf16[384,512]{1,0:T(8,128)(2,1)}, u32[]{:S(2)}, u32[]{:S(2)}) collective-permute-start(bf16[384,512]{1,0:T(8,128)(2,1)} %bitcast.7.refs_0_), channel_id=1, source_target_pairs={{0,8},{4,12},{8,0},{12,4},{1,9},{5,13},{9,1},{13,5},{2,10},{6,14},... | collective-permute-start | bytes 1179656 | tf_op jit(solution)/shard_map/ppermute | solution.py:516
  25.6 9.8 %collective-permute-start = (bf16[384,512]{1,0:T(8,128)(2,1)}, bf16[384,512]{1,0:T(8,128)(2,1)}, u32[]{:S(2)}, u32[]{:S(2)}) collective-permute-start(bf16[384,512]{1,0:T(8,128)(2,1)} %bitcast.7.refs_0_), channel_id=1, source_target_pairs={{0,4},{4,0},{8,12},{12,8},{1,5},{5,1},{9,13},{13,9},{2,6},{6,2},{1... | collective-permute-start | bytes 1179656 | tf_op jit(solution)/shard_map/ppermute | solution.py:516
  25.8 15.6 %collective-permute-start.7 = (bf16[12,208,512]{2,1,0:T(8,128)(2,1)}, bf16[12,208,512]{2,1,0:T(8,128)(2,1)}, u32[]{:S(2)}, u32[]{:S(2)}) collective-permute-start(bf16[12,208,512]{2,1,0:T(8,128)(2,1)} %pad.21.refs_8_), channel_id=1, source_target_pairs={{0,16},{16,0},{1,17},{17,1},{2,18},{18,2},{3,19},{19,3},{4,20},{20... | collective-permute-start | bytes 7667720 | tf_op jit(solution)/shard_map/ppermute | solution.py:512
  37.8 18.9 %collective-permute-start.15 = (bf16[576,512]{1,0:T(8,128)(2,1)S(1)}, bf16[576,512]{1,0:T(8,128)(2,1)S(1)}, u32[]{:S(2)}, u32[]{:S(2)}) collective-permute-start(bf16[576,512]{1,0:T(8,128)(2,1)S(1)} %get-tuple-element.127.refs_0_), channel_id=1, source_target_pairs={{0,12},{4,8},{8,4},{12,0},{1,13},{5,9},{9,5},{13,1},{2,14},{6,10},... | collective-permute-start | bytes 1769480 | tf_op jit(solution)/shard_map/ppermute | solution.py:516
  40.1 26.5 %collective-permute-start.14 = (bf16[576,512]{1,0:T(8,128)(2,1)S(1)}, bf16[576,512]{1,0:T(8,128)(2,1)S(1)}, u32[]{:S(2)}, u32[]{:S(2)}) collective-permute-start(bf16[576,512]{1,0:T(8,128)(2,1)S(1)} %get-tuple-element.127.refs_0_), channel_id=1, source_target_pairs={{0,8},{4,12},{8,0},{12,4},{1,9},{5,13},{9,1},{13,5},{2,10},{6,14},... | collective-permute-start | bytes 1769480 | tf_op jit(solution)/shard_map/ppermute | solution.py:516
  40.6 26.1 %collective-permute-start.13 = (bf16[576,512]{1,0:T(8,128)(2,1)S(1)}, bf16[576,512]{1,0:T(8,128)(2,1)S(1)}, u32[]{:S(2)}, u32[]{:S(2)}) collective-permute-start(bf16[576,512]{1,0:T(8,128)(2,1)S(1)} %get-tuple-element.127.refs_0_), channel_id=1, source_target_pairs={{0,4},{4,0},{8,12},{12,8},{1,5},{5,1},{9,13},{13,9},{2,6},{6,2},{1... | collective-permute-start | bytes 1769480 | tf_op jit(solution)/shard_map/ppermute | solution.py:516
  69.0 23.7 %collective-permute-start.22 = (bf16[576,512]{1,0:T(8,128)(2,1)S(1)}, bf16[576,512]{1,0:T(8,128)(2,1)S(1)}, u32[]{:S(2)}, u32[]{:S(2)}) collective-permute-start(bf16[576,512]{1,0:T(8,128)(2,1)S(1)} %get-tuple-element.135.refs_0_), channel_id=1, source_target_pairs={{0,12},{4,8},{8,4},{12,0},{1,13},{5,9},{9,5},{13,1},{2,14},{6,10},... | collective-permute-start | bytes 1769480 | tf_op jit(solution)/shard_map/ppermute | solution.py:516
  70.7 27.1 %collective-permute-start.21 = (bf16[576,512]{1,0:T(8,128)(2,1)S(1)}, bf16[576,512]{1,0:T(8,128)(2,1)S(1)}, u32[]{:S(2)}, u32[]{:S(2)}) collective-permute-start(bf16[576,512]{1,0:T(8,128)(2,1)S(1)} %get-tuple-element.135.refs_0_), channel_id=1, source_target_pairs={{0,8},{4,12},{8,0},{12,4},{1,9},{5,13},{9,1},{13,5},{2,10},{6,14},... | collective-permute-start | bytes 1769480 | tf_op jit(solution)/shard_map/ppermute | solution.py:516
  71.9 26.0 %collective-permute-start.20 = (bf16[576,512]{1,0:T(8,128)(2,1)S(1)}, bf16[576,512]{1,0:T(8,128)(2,1)S(1)}, u32[]{:S(2)}, u32[]{:S(2)}) collective-permute-start(bf16[576,512]{1,0:T(8,128)(2,1)S(1)} %get-tuple-element.135.refs_0_), channel_id=1, source_target_pairs={{0,4},{4,0},{8,12},{12,8},{1,5},{5,1},{9,13},{13,9},{2,6},{6,2},{1... | collective-permute-start | bytes 1769480 | tf_op jit(solution)/shard_map/ppermute | solution.py:516
  97.9 15.5 %collective-permute-start.23 = (bf16[576,512]{1,0:T(8,128)(2,1)S(1)}, bf16[576,512]{1,0:T(8,128)(2,1)S(1)}, u32[]{:S(2)}, u32[]{:S(2)}) collective-permute-start(bf16[576,512]{1,0:T(8,128)(2,1)S(1)} %get-tuple-element.135.refs_0_), channel_id=1, source_target_pairs={{0,16},{16,0},{1,17},{17,1},{2,18},{18,2},{3,19},{19,3},{4,20},{20... | collective-permute-start | bytes 1769480 | tf_op jit(solution)/shard_map/ppermute | solution.py:512
  97.9 15.5 %collective-permute-start.24 = (bf16[576,512]{1,0:T(8,128)(2,1)S(1)}, bf16[576,512]{1,0:T(8,128)(2,1)S(1)}, u32[]{:S(2)}, u32[]{:S(2)}) collective-permute-start(bf16[576,512]{1,0:T(8,128)(2,1)S(1)} %collective-permute-done.20.refs_1_), channel_id=1, source_target_pairs={{0,16},{16,0},{1,17},{17,1},{2,18},{18,2},{3,19},{19,3},{4,20},{20... | collective-permute-start | bytes 1769480 | tf_op jit(solution)/shard_map/ppermute | solution.py:512
  98.4 15.0 %collective-permute-start.25 = (bf16[576,512]{1,0:T(8,128)(2,1)S(1)}, bf16[576,512]{1,0:T(8,128)(2,1)S(1)}, u32[]{:S(2)}, u32[]{:S(2)}) collective-permute-start(bf16[576,512]{1,0:T(8,128)(2,1)S(1)} %collective-permute-done.21.refs_2_), channel_id=1, source_target_pairs={{0,16},{16,0},{1,17},{17,1},{2,18},{18,2},{3,19},{19,3},{4,20},{20... | collective-permute-start | bytes 1769480 | tf_op jit(solution)/shard_map/ppermute | solution.py:512
  98.5 14.9 %collective-permute-start.26 = (bf16[576,512]{1,0:T(8,128)(2,1)S(1)}, bf16[576,512]{1,0:T(8,128)(2,1)S(1)}, u32[]{:S(2)}, u32[]{:S(2)}) collective-permute-start(bf16[576,512]{1,0:T(8,128)(2,1)S(1)} %collective-permute-done.22.refs_3_), channel_id=1, source_target_pairs={{0,16},{16,0},{1,17},{17,1},{2,18},{18,2},{3,19},{19,3},{4,20},{20... | collective-permute-start | bytes 1769480 | tf_op jit(solution)/shard_map/ppermute | solution.py:512
  166.5 24.6 %collective-permute-start.30 = (bf16[576,512]{1,0:T(8,128)(2,1)S(1)}, bf16[576,512]{1,0:T(8,128)(2,1)}, u32[]{:S(2)}, u32[]{:S(2)}) collective-permute-start(bf16[576,512]{1,0:T(8,128)(2,1)S(1)} %get-tuple-element.270), channel_id=1, source_target_pairs={{0,12},{4,8},{8,4},{12,0},{1,13},{5,9},{9,5},{13,1},{2,14},{6,10},... | collective-permute-start | bytes 1769480 | tf_op jit(solution)/shard_map/ppermute | solution.py:516
  168.3 27.3 %collective-permute-start.29 = (bf16[576,512]{1,0:T(8,128)(2,1)S(1)}, bf16[576,512]{1,0:T(8,128)(2,1)}, u32[]{:S(2)}, u32[]{:S(2)}) collective-permute-start(bf16[576,512]{1,0:T(8,128)(2,1)S(1)} %get-tuple-element.271), channel_id=1, source_target_pairs={{0,8},{4,12},{8,0},{12,4},{1,9},{5,13},{9,1},{13,5},{2,10},{6,14},... | collective-permute-start | bytes 1769480 | tf_op jit(solution)/shard_map/ppermute | solution.py:516
  169.4 26.2 %collective-permute-start.28 = (bf16[576,512]{1,0:T(8,128)(2,1)S(1)}, bf16[576,512]{1,0:T(8,128)(2,1)}, u32[]{:S(2)}, u32[]{:S(2)}) collective-permute-start(bf16[576,512]{1,0:T(8,128)(2,1)S(1)} %get-tuple-element.272), channel_id=1, source_target_pairs={{0,4},{4,0},{8,12},{12,8},{1,5},{5,1},{9,13},{13,9},{2,6},{6,2},{1... | collective-permute-start | bytes 1769480 | tf_op jit(solution)/shard_map/ppermute | solution.py:516
  195.6 8.2 %collective-permute-start.31 = (bf16[4,192,512]{2,1,0:T(8,128)(2,1)}, bf16[4,192,512]{2,1,0:T(8,128)(2,1)}, u32[]{:S(2)}, u32[]{:S(2)}) collective-permute-start(bf16[4,192,512]{2,1,0:T(8,128)(2,1)} %get-tuple-element.157), channel_id=1, source_target_pairs={{0,16},{16,0},{1,17},{17,1},{2,18},{18,2},{3,19},{19,3},{4,20},{20... | collective-permute-start | bytes 2359304 | tf_op jit(solution)/shard_map/ppermute | solution.py:512
  201.2 32.9 %collective-permute-start.32 = (bf16[576,512]{1,0:T(8,128)(2,1)S(1)}, bf16[576,512]{1,0:T(8,128)(2,1)S(1)}, u32[]{:S(2)}, u32[]{:S(2)}) collective-permute-start(bf16[576,512]{1,0:T(8,128)(2,1)S(1)} %fusion.21), channel_id=1, source_target_pairs={{0,2},{1,3},{2,0},{3,1},{4,6},{5,7},{6,4},{7,5},{8,10},{9,11},{10,... | collective-permute-start | bytes 1769480 | tf_op jit(solution)/shard_map/ppermute | solution.py:521
  205.1 29.0 %collective-permute-start.35 = (bf16[192,512]{1,0:T(8,128)(2,1)S(1)}, bf16[192,512]{1,0:T(8,128)(2,1)S(1)}, u32[]{:S(2)}, u32[]{:S(2)}) collective-permute-start(bf16[192,512]{1,0:T(8,128)(2,1)S(1)} %get-tuple-element.282), channel_id=1, source_target_pairs={{0,12},{4,8},{8,4},{12,0},{1,13},{5,9},{9,5},{13,1},{2,14},{6,10},... | collective-permute-start | bytes 589832 | tf_op jit(solution)/shard_map/ppermute | solution.py:516
  206.9 27.3 %collective-permute-start.34 = (bf16[192,512]{1,0:T(8,128)(2,1)S(1)}, bf16[192,512]{1,0:T(8,128)(2,1)S(1)}, u32[]{:S(2)}, u32[]{:S(2)}) collective-permute-start(bf16[192,512]{1,0:T(8,128)(2,1)S(1)} %get-tuple-element.283), channel_id=1, source_target_pairs={{0,8},{4,12},{8,0},{12,4},{1,9},{5,13},{9,1},{13,5},{2,10},{6,14},... | collective-permute-start | bytes 589832 | tf_op jit(solution)/shard_map/ppermute | solution.py:516
  208.0 26.1 %collective-permute-start.33 = (bf16[192,512]{1,0:T(8,128)(2,1)S(1)}, bf16[192,512]{1,0:T(8,128)(2,1)S(1)}, u32[]{:S(2)}, u32[]{:S(2)}) collective-permute-start(bf16[192,512]{1,0:T(8,128)(2,1)S(1)} %get-tuple-element.284), channel_id=1, source_target_pairs={{0,4},{4,0},{8,12},{12,8},{1,5},{5,1},{9,13},{13,9},{2,6},{6,2},{1... | collective-permute-start | bytes 589832 | tf_op jit(solution)/shard_map/ppermute | solution.py:516
  235.4 29.5 %collective-permute-start.38 = (bf16[192,512]{1,0:T(8,128)(2,1)S(1)}, bf16[192,512]{1,0:T(8,128)(2,1)S(1)}, u32[]{:S(2)}, u32[]{:S(2)}) collective-permute-start(bf16[192,512]{1,0:T(8,128)(2,1)S(1)} %fusion.35), channel_id=1, source_target_pairs={{0,1},{1,0},{2,3},{3,2},{4,5},{5,4},{6,7},{7,6},{8,9},{9,8},{10,11... | collective-permute-start | bytes 589832 | tf_op jit(solution)/shard_map/ppermute | solution.py:521
  237.2 27.7 %collective-permute-start.37 = (bf16[576,512]{1,0:T(8,128)(2,1)S(1)}, bf16[576,512]{1,0:T(8,128)(2,1)S(1)}, u32[]{:S(2)}, u32[]{:S(2)}) collective-permute-start(bf16[576,512]{1,0:T(8,128)(2,1)S(1)} %add_convert_fusion.7), channel_id=1, source_target_pairs={{0,1},{1,0},{2,3},{3,2},{4,5},{5,4},{6,7},{7,6},{8,9},{9,8},{10,11... | collective-permute-start | bytes 1769480 | tf_op jit(solution)/shard_map/ppermute | solution.py:521
  240.4 24.5 %collective-permute-start.41 = (bf16[576,512]{1,0:T(8,128)(2,1)}, bf16[576,512]{1,0:T(8,128)(2,1)S(1)}, u32[]{:S(2)}, u32[]{:S(2)}) collective-permute-start(bf16[576,512]{1,0:T(8,128)(2,1)} %get-tuple-element.267), channel_id=1, source_target_pairs={{0,12},{4,8},{8,4},{12,0},{1,13},{5,9},{9,5},{13,1},{2,14},{6,10},... | collective-permute-start | bytes 1769480 | tf_op jit(solution)/shard_map/ppermute | solution.py:516
  242.1 27.4 %collective-permute-start.40 = (bf16[576,512]{1,0:T(8,128)(2,1)}, bf16[576,512]{1,0:T(8,128)(2,1)S(1)}, u32[]{:S(2)}, u32[]{:S(2)}) collective-permute-start(bf16[576,512]{1,0:T(8,128)(2,1)} %get-tuple-element.268), channel_id=1, source_target_pairs={{0,8},{4,12},{8,0},{12,4},{1,9},{5,13},{9,1},{13,5},{2,10},{6,14},... | collective-permute-start | bytes 1769480 | tf_op jit(solution)/shard_map/ppermute | solution.py:516
  243.3 26.3 %collective-permute-start.39 = (bf16[576,512]{1,0:T(8,128)(2,1)}, bf16[576,512]{1,0:T(8,128)(2,1)S(1)}, u32[]{:S(2)}, u32[]{:S(2)}) collective-permute-start(bf16[576,512]{1,0:T(8,128)(2,1)} %get-tuple-element.269), channel_id=1, source_target_pairs={{0,4},{4,0},{8,12},{12,8},{1,5},{5,1},{9,13},{13,9},{2,6},{6,2},{1... | collective-permute-start | bytes 1769480 | tf_op jit(solution)/shard_map/ppermute | solution.py:516
  269.6 6.6 %collective-permute-start.42 = (bf16[4,192,512]{2,1,0:T(8,128)(2,1)}, bf16[4,192,512]{2,1,0:T(8,128)(2,1)S(1)}, u32[]{:S(2)}, u32[]{:S(2)}) collective-permute-start(bf16[4,192,512]{2,1,0:T(8,128)(2,1)} %get-tuple-element.196), channel_id=1, source_target_pairs={{0,16},{16,0},{1,17},{17,1},{2,18},{18,2},{3,19},{19,3},{4,20},{20... | collective-permute-start | bytes 2359304 | tf_op jit(solution)/shard_map/ppermute | solution.py:512
  271.2 25.7 %collective-permute-start.47 = (bf16[192,512]{1,0:T(8,128)(2,1)S(1)}, bf16[192,512]{1,0:T(8,128)(2,1)}, u32[]{:S(2)}, u32[]{:S(2)}) collective-permute-start(bf16[192,512]{1,0:T(8,128)(2,1)S(1)} %add_convert_fusion.16), channel_id=1, source_target_pairs={{0,2},{1,3},{2,0},{3,1},{4,6},{5,7},{6,4},{7,5},{8,10},{9,11},{10,... | collective-permute-start | bytes 589832 | tf_op jit(solution)/shard_map/ppermute | solution.py:521
  273.5 35.1 %collective-permute-start.46 = (bf16[576,512]{1,0:T(8,128)(2,1)S(1)}, bf16[576,512]{1,0:T(8,128)(2,1)}, u32[]{:S(2)}, u32[]{:S(2)}) collective-permute-start(bf16[576,512]{1,0:T(8,128)(2,1)S(1)} %fusion.18), channel_id=1, source_target_pairs={{0,2},{1,3},{2,0},{3,1},{4,6},{5,7},{6,4},{7,5},{8,10},{9,11},{10,... | collective-permute-start | bytes 1769480 | tf_op jit(solution)/shard_map/ppermute | solution.py:521
  282.9 25.7 %collective-permute-start.45 = (bf16[192,512]{1,0:T(8,128)(2,1)}, bf16[192,512]{1,0:T(8,128)(2,1)}, u32[]{:S(2)}, u32[]{:S(2)}) collective-permute-start(bf16[192,512]{1,0:T(8,128)(2,1)} %get-tuple-element.279), channel_id=1, source_target_pairs={{0,12},{4,8},{8,4},{12,0},{1,13},{5,9},{9,5},{13,1},{2,14},{6,10},... | collective-permute-start | bytes 589832 | tf_op jit(solution)/shard_map/ppermute | solution.py:516
  284.5 24.1 %collective-permute-start.44 = (bf16[192,512]{1,0:T(8,128)(2,1)}, bf16[192,512]{1,0:T(8,128)(2,1)}, u32[]{:S(2)}, u32[]{:S(2)}) collective-permute-start(bf16[192,512]{1,0:T(8,128)(2,1)} %get-tuple-element.280), channel_id=1, source_target_pairs={{0,8},{4,12},{8,0},{12,4},{1,9},{5,13},{9,1},{13,5},{2,10},{6,14},... | collective-permute-start | bytes 589832 | tf_op jit(solution)/shard_map/ppermute | solution.py:516
  285.7 22.9 %collective-permute-start.43 = (bf16[192,512]{1,0:T(8,128)(2,1)}, bf16[192,512]{1,0:T(8,128)(2,1)}, u32[]{:S(2)}, u32[]{:S(2)}) collective-permute-start(bf16[192,512]{1,0:T(8,128)(2,1)} %get-tuple-element.281), channel_id=1, source_target_pairs={{0,4},{4,0},{8,12},{12,8},{1,5},{5,1},{9,13},{13,9},{2,6},{6,2},{1... | collective-permute-start | bytes 589832 | tf_op jit(solution)/shard_map/ppermute | solution.py:516
  296.9 28.6 %collective-permute-start.49 = (bf16[12,208,512]{2,1,0:T(8,128)(2,1)S(1)}, bf16[12,208,512]{2,1,0:T(8,128)(2,1)S(1)}, u32[]{:S(2)}, u32[]{:S(2)}) collective-permute-start(bf16[12,208,512]{2,1,0:T(8,128)(2,1)S(1)} %copy-done.4), channel_id=1, source_target_pairs={{0,16},{1,17},{2,18},{3,19},{4,20},{5,21},{6,22},{7,23},{8,24},{9,... | collective-permute-start | bytes 7667720 | tf_op jit(solution)/shard_map/ppermute | solution.py:723
  308.6 17.6 %collective-permute-start.48 = (bf16[12,208,512]{2,1,0:T(8,128)(2,1)}, bf16[12,208,512]{2,1,0:T(8,128)(2,1)S(1)}, u32[]{:S(2)}, u32[]{:S(2)}) collective-permute-start(bf16[12,208,512]{2,1,0:T(8,128)(2,1)} %get-tuple-element.209), channel_id=1, source_target_pairs={{16,0},{17,1},{18,2},{19,3},{20,4},{21,5},{22,6},{23,7},{24,8},{25... | collective-permute-start | bytes 7667720 | tf_op jit(solution)/shard_map/ppermute | solution.py:779
  311.3 6.9 %collective-permute-start.51 = (f32[144,128]{1,0:T(8,128)S(1)}, f32[144,128]{1,0:T(8,128)S(1)}, u32[]{:S(2)}, u32[]{:S(2)}) collective-permute-start(f32[144,128]{1,0:T(8,128)S(1)} %reshape.331), channel_id=1, source_target_pairs={{0,16},{16,0},{1,17},{17,1},{2,18},{18,2},{3,19},{19,3},{4,20},{20... | collective-permute-start | bytes 221192 | tf_op jit(solution)/shard_map/ppermute | solution.py:512
  314.1 7.8 %collective-permute-start.50 = (bf16[192,512]{1,0:T(8,128)(2,1)S(1)}, bf16[192,512]{1,0:T(8,128)(2,1)S(1)}, u32[]{:S(2)}, u32[]{:S(2)}) collective-permute-start(bf16[192,512]{1,0:T(8,128)(2,1)S(1)} %fusion.32), channel_id=1, source_target_pairs={{0,1},{1,0},{2,3},{3,2},{4,5},{5,4},{6,7},{7,6},{8,9},{9,8},{10,11... | collective-permute-start | bytes 589832 | tf_op jit(solution)/shard_map/ppermute | solution.py:521
  316.3 24.1 %collective-permute-start.56 = (bf16[576,512]{1,0:T(8,128)(2,1)}, bf16[576,512]{1,0:T(8,128)(2,1)}, u32[]{:S(2)}, u32[]{:S(2)}) collective-permute-start(bf16[576,512]{1,0:T(8,128)(2,1)} %add_convert_fusion.2), channel_id=1, source_target_pairs={{0,1},{1,0},{2,3},{3,2},{4,5},{5,4},{6,7},{7,6},{8,9},{9,8},{10,11... | collective-permute-start | bytes 1769480 | tf_op jit(solution)/shard_map/ppermute | solution.py:521
  321.9 8.9 %collective-permute-start.54 = (f32[144,128]{1,0:T(8,128)S(1)}, f32[144,128]{1,0:T(8,128)S(1)}, u32[]{:S(2)}, u32[]{:S(2)}) collective-permute-start(f32[144,128]{1,0:T(8,128)S(1)} %add.223), channel_id=1, source_target_pairs={{0,12},{4,8},{8,4},{12,0},{1,13},{5,9},{9,5},{13,1},{2,14},{6,10},... | collective-permute-start | bytes 221192 | tf_op jit(solution)/shard_map/ppermute | solution.py:516
  323.6 7.2 %collective-permute-start.53 = (f32[144,128]{1,0:T(8,128)S(1)}, f32[144,128]{1,0:T(8,128)}, u32[]{:S(2)}, u32[]{:S(2)}) collective-permute-start(f32[144,128]{1,0:T(8,128)S(1)} %add.223), channel_id=1, source_target_pairs={{0,8},{4,12},{8,0},{12,4},{1,9},{5,13},{9,1},{13,5},{2,10},{6,14},... | collective-permute-start | bytes 221192 | tf_op jit(solution)/shard_map/ppermute | solution.py:516
  326.2 14.2 %collective-permute-start.55 = (bf16[192,512]{1,0:T(8,128)(2,1)}, bf16[192,512]{1,0:T(8,128)(2,1)}, u32[]{:S(2)}, u32[]{:S(2)}) collective-permute-start(bf16[192,512]{1,0:T(8,128)(2,1)} %add_convert_fusion.14), channel_id=1, source_target_pairs={{0,2},{1,3},{2,0},{3,1},{4,6},{5,7},{6,4},{7,5},{8,10},{9,11},{10,... | collective-permute-start | bytes 589832 | tf_op jit(solution)/shard_map/ppermute | solution.py:521
  331.8 8.6 %collective-permute-start.59 = (f32[144,128]{1,0:T(8,128)S(1)}, f32[144,128]{1,0:T(8,128)S(1)}, u32[]{:S(2)}, u32[]{:S(2)}) collective-permute-start(f32[144,128]{1,0:T(8,128)S(1)} %add_add_fusion.1), channel_id=1, source_target_pairs={{0,3},{1,2},{2,1},{3,0},{4,7},{5,6},{6,5},{7,4},{8,11},{9,10},{10,... | collective-permute-start | bytes 221192 | tf_op jit(solution)/shard_map/ppermute | solution.py:521
  334.0 9.5 %collective-permute-start.58 = (f32[144,128]{1,0:T(8,128)S(1)}, f32[144,128]{1,0:T(8,128)S(1)}, u32[]{:S(2)}, u32[]{:S(2)}) collective-permute-start(f32[144,128]{1,0:T(8,128)S(1)} %add_add_fusion.1), channel_id=1, source_target_pairs={{0,2},{1,3},{2,0},{3,1},{4,6},{5,7},{6,4},{7,5},{8,10},{9,11},{10,... | collective-permute-start | bytes 221192 | tf_op jit(solution)/shard_map/ppermute | solution.py:521
  335.1 9.1 %collective-permute-start.57 = (f32[144,128]{1,0:T(8,128)S(1)}, f32[144,128]{1,0:T(8,128)}, u32[]{:S(2)}, u32[]{:S(2)}) collective-permute-start(f32[144,128]{1,0:T(8,128)S(1)} %add_add_fusion.1), channel_id=1, source_target_pairs={{0,1},{1,0},{2,3},{3,2},{4,5},{5,4},{6,7},{7,6},{8,9},{9,8},{10,11... | collective-permute-start | bytes 221192 | tf_op jit(solution)/shard_map/ppermute | solution.py:521
  348.0 7.4 %collective-permute-start.60 = (bf16[768,512]{1,0:T(8,128)(2,1)}, bf16[768,512]{1,0:T(8,128)(2,1)}, u32[]{:S(2)}, u32[]{:S(2)}) collective-permute-start(bf16[768,512]{1,0:T(8,128)(2,1)} %broadcast_select_fusion), channel_id=1, source_target_pairs={{0,16},{16,0},{1,17},{17,1},{2,18},{18,2},{3,19},{19,3},{4,20},{20... | collective-permute-start | bytes 2359304 | tf_op jit(solution)/shard_map/ppermute | solution.py:512
  (77 other events, 554.2 us)

commit v2 on v1

--- a/solution.py
+++ b/solution.py
@@ -5,6 +5,7 @@
 import numpy as np
 from jax import lax
 from jax.experimental import pallas as pl
+from jax.experimental.layout import Layout, with_layout_constraint
 from jax.experimental.pallas import tpu as pltpu
 from jax.sharding import PartitionSpec as P
 
@@ -283,7 +284,7 @@
         g = pick(info, 1, g_refs)
         cols = [slice(512 * c, 512 * c + 512) for c in range(4)]
         for c in cols:
-            accumulate(d_down, (c, slice(None)), mm_tn(act_ref[0, :, c], g))
+            accumulate(d_down, (slice(None), c), mm_tn(g, act_ref[0, :, c]))
         add_row(vec_out, 7, g.astype(F32))
         xhat, inverse = standard(mid_ref[0])
         normed_two = (xhat * vec_ref[1:2] + vec_ref[6:7]).astype(BF16)
@@ -314,7 +315,7 @@
                         rows, 512 * c : 512 * c + 512
                     ].astype(BF16)
                 deep = pl.ds(pl.multiple_of(512 * shard + 256 * half, 256), 256)
-                out_ref[at, 256:512, :] = d_down[deep, :].astype(BF16)
+                out_ref[at, 256:512, :] = d_down[:, deep].T.astype(BF16)
                 out_ref[at, 512:576, :] = d_out[rows, :].astype(BF16)
 
 
@@ -481,7 +482,7 @@
         [MID, X],
         [((4, 576, 512), BF16)] * 2 + [VEC, ((1, 2048), F32)],
         MLP_WEIGHTS
-        + [pltpu.VMEM((512, 512), F32), pltpu.VMEM((512, 2048), F32), pltpu.VMEM((2048, 512), F32)],
+        + [pltpu.VMEM((512, 512), F32), pltpu.VMEM((512, 2048), F32), pltpu.VMEM((512, 2048), F32)],
         30,
     )
 
@@ -785,6 +786,7 @@
     chosen = jnp.where(present[:, None, None], chosen, jnp.zeros((), BF16))[:, :TOKENS]
     results = chosen.reshape(1, mb_count, per_device, SIDE, SIDE, 512)
     boundary_of((), [first_attn, small_flow])
+    results = with_layout_constraint(results, Layout(major_to_minor=(0, 2, 3, 4, 1, 5)))
     results = boundary_of(results, [small_flow])
     boundary_of((), [first_attn, first_mlp, small_flow])
     flows = [first_attn, small_flow, first_mlp, second_attn, second_mlp]

time: 369 us -> 365 us (0.989)
    unnamed x136 -> x131, local copies, waits for them, and re-layouts: 14.5 us -> 9.94 us
    reshape x1 -> x2, local copies, waits for them, and re-layouts: 2.73 us -> 6.45 us  [body(): results = chosen.reshape(1, mb_count, per_device, SIDE, SIDE, 512)]
  transfers between devices with their start and end apart: 61 -> 61, of which waited for: 16 -> 17; matrix products, arithmetic and copies ran while one was open for 16% -> 16% of each run, Pallas kernels for 32% -> 32%
where the time goes in v2:
time: 365 us; the launch traced here: 361 us
  Pallas kernels  161 us (44%)
  waiting for transfers between devices  60.8 us (17%)
  starting transfers between devices  55.3 us (15%)
  local copies, waits for them, and re-layouts  41.4 us (11%)
  other arithmetic  34.3 us (9%)
  matrix products  5.16 us (1%)
    pallas_call x8, Pallas kernels, run(): pl.pallas_call(kernel, grid_spec=pltpu.PrefetchScalarGridSpec(num_scalar_...  161 us
    ppermute x27, starting transfers between devices, across(): return lax.ppermute(block, 'shard', [(i, i ^ distance) for i in range(4)])  32.7 us
    ppermute x11, waiting for transfers between devices, along(): lax.ppermute(block, 'replica', [(i, i ^ distance) for i in range(size)])  26.8 us
    ppermute x27, waiting for transfers between devices, across(): return lax.ppermute(block, 'shard', [(i, i ^ distance) for i in range(4)])  24.9 us
    convert_element_type x16, other arithmetic, add_low(): return total.astype(BF16)  22.3 us
    ppermute x11, starting transfers between devices, along(): lax.ppermute(block, 'replica', [(i, i ^ distance) for i in range(size)])  14.3 us
    unnamed x131, local copies, waits for them, and re-layouts  9.94 us
    ppermute x21, waiting for transfers between devices, swap(): return lax.ppermute(block, 'section', [(0, 1), (1, 0)])  9 us
  transfers between devices with their start and end apart: 61, of which 17 were waited for; matrix products, arithmetic and copies ran while one was open for 16% of the time, Pallas kernels for 32%

profile of v2, /device:TPU:0, one launch (start us, length us, event | category | flops | bytes accessed | tf_op | source)
XLA Modules:
  0.0 361.1 jit_solution(12638209509738170218)
XLA Ops:
  4.0 3.0 collective-permute-start.10
  7.0 1.4 collective-permute-start.9
  8.5 2.9 collective-permute-start.2
  17.1 2.3 copy.64
  19.4 2.8 reshape.315
  22.2 3.4 pad.21.refs_8_
  27.1 3.1 collective-permute-done.11
  37.7 2.3 collective-permute-start.15
  42.0 14.6 %shard_map.205 = (bf16[6,256,1536]{2,1,0:T(8,128)(2,1)}, bf16[6,4,4,64,256]{4,3,2,1,0:T(8,128)(2,1)}, bf16[6,208,512]{2,1,0:T(8,128)(2,1)}, bf16[6,208,512]{2,1,0:T(8,128)(2,1)}) custom-call(s32[9]{0:T(128)} %pad_add_fusion.info, bf16[384,512]{1,0:T(8,128)(2,1)} %bitcast.7.refs_0_, bf16[384,512]{1,0:T(8,128)(2,1)} %collective-permute-done.refs_1_, ...), custom_call_target="tpu_custom_call" | custom-call | flops 20000000000 | bytes 20000000 | tf_op jit(solution)/shard_map/pallas_call | solution.py:419
  56.7 9.9 %collective-permute-done.14.refs_2_ = bf16[576,512]{1,0:T(8,128)(2,1)S(1)} collective-permute-done((bf16[576,512]{1,0:T(8,128)(2,1)S(1)}, bf16[576,512]{1,0:T(8,128)(2,1)S(1)}, u32[]{:S(2)}, u32[]{:S(2)}) %collective-permute-start.14) | collective-permute-done | bytes 589856 | tf_op jit(solution)/shard_map/ppermute | solution.py:517
  68.9 1.7 collective-permute-start.22
  73.4 19.2 %shard_map.206 = (bf16[6,208,512]{2,1,0:T(8,128)(2,1)}, f32[6,208,512]{2,1,0:T(8,128)}, bf16[6,208,2048]{2,1,0:T(8,128)(2,1)}, bf16[6,208,2048]{2,1,0:T(8,128)(2,1)}) custom-call(s32[9]{0:T(128)} %pad_add_fusion.info, bf16[576,512]{1,0:T(8,128)(2,1)} %copy-done.15, bf16[576,512]{1,0:T(8,128)(2,1)} %copy-done.45, bf16[576,512]{1,0:T(8,128)(2,1)} %copy-done.44, ...), custom_call_target="tpu_custom_call" | custom-call | flops 20000000000 | bytes 20000000 | tf_op jit(solution)/shard_map/pallas_call | solution.py:419
  92.7 5.1 %collective-permute-done.21.refs_2_ = bf16[576,512]{1,0:T(8,128)(2,1)S(1)} collective-permute-done((bf16[576,512]{1,0:T(8,128)(2,1)S(1)}, bf16[576,512]{1,0:T(8,128)(2,1)S(1)}, u32[]{:S(2)}, u32[]{:S(2)}) %collective-permute-start.21) | collective-permute-done | bytes 589856 | tf_op jit(solution)/shard_map/ppermute | solution.py:517
  98.9 14.4 %shard_map.207 = (bf16[6,256,1536]{2,1,0:T(8,128)(2,1)}, bf16[6,4,4,64,256]{4,3,2,1,0:T(8,128)(2,1)}, bf16[6,208,512]{2,1,0:T(8,128)(2,1)}) custom-call(s32[9]{0:T(128)} %pad_add_fusion.info, bf16[384,512]{1,0:T(8,128)(2,1)} %bitcast.7.refs_0_, bf16[384,512]{1,0:T(8,128)(2,1)} %collective-permute-done.refs_1_, ...), custom_call_target="tpu_custom_call" | custom-call | flops 20000000000 | bytes 20000000 | tf_op jit(solution)/shard_map/pallas_call | solution.py:419
  114.7 19.3 %shard_map.208 = (bf16[12,208,512]{2,1,0:T(8,128)(2,1)}, f32[6,208,512]{2,1,0:T(8,128)}, bf16[6,208,2048]{2,1,0:T(8,128)(2,1)}, bf16[6,208,2048]{2,1,0:T(8,128)(2,1)}) custom-call(s32[9]{0:T(128)} %pad_add_fusion.info, bf16[576,512]{1,0:T(8,128)(2,1)} %copy-done.16, bf16[576,512]{1,0:T(8,128)(2,1)} %copy-done.52, bf16[576,512]{1,0:T(8,128)(2,1)} %copy-done.51, ...), custom_call_target="tpu_custom_call" | custom-call | flops 20000000000 | bytes 20000000 | tf_op jit(solution)/shard_map/pallas_call | solution.py:419
  134.1 26.0 %shard_map.209 = (f32[6,208,512]{2,1,0:T(8,128)}, bf16[6,208,512]{2,1,0:T(8,128)(2,1)}, bf16[4,576,512]{2,1,0:T(8,128)(2,1)}, bf16[4,576,512]{2,1,0:T(8,128)(2,1)}, f32[8,512]{1,0:T(8,128)}, /*index=5*/f32[1,2048]{1,0:T(1,128)}) custom-call(s32[9]{0:T(128)} %pad_add_fusion.info, bf16[576,512]{1,0:T(8,128)(2,1)} %copy-done.16, bf16[576,512]{1,0:T(8,128)(2,1)} %copy-done.52, ...), custom_call_target="tpu_custom_call" | custom-call | flops 30000001024 | bytes 30000000 | tf_op jit(solution)/shard_map/pallas_call | solution.py:419
  160.2 4.7 %collective-permute-done.27 = bf16[4,576,512]{2,1,0:T(8,128)(2,1)S(1)} collective-permute-done((bf16[4,576,512]{2,1,0:T(8,128)(2,1)}, bf16[4,576,512]{2,1,0:T(8,128)(2,1)S(1)}, u32[]{:S(2)}, u32[]{:S(2)}) %collective-permute-start.27) | collective-permute-done | bytes 2359328 | tf_op jit(solution)/shard_map/ppermute | solution.py:513
  164.8 1.9 fusion.24
  166.8 1.8 collective-permute-start.30
  170.3 21.1 %shard_map.210 = (bf16[6,208,512]{2,1,0:T(8,128)(2,1)}, bf16[4,192,512]{2,1,0:T(8,128)(2,1)}, bf16[4,192,512]{2,1,0:T(8,128)(2,1)}, f32[8,512]{1,0:T(8,128)}, f32[16,64,64]{2,1,0:T(8,128)}) custom-call(s32[9]{0:T(128)} %pad_add_fusion.info, bf16[384,512]{1,0:T(8,128)(2,1)} %bitcast.7.refs_0_, bf16[384,512]{1,0:T(8,128)(2,1)} %collective-permute-done.refs_1_, ...), custom_call_target="tpu_custom_call" | custom-call | flops 30000001024 | bytes 30000000 | tf_op jit(solution)/shard_map/pallas_call | solution.py:419
  191.4 4.4 %collective-permute-done.29 = bf16[576,512]{1,0:T(8,128)(2,1)} collective-permute-done((bf16[576,512]{1,0:T(8,128)(2,1)S(1)}, bf16[576,512]{1,0:T(8,128)(2,1)}, u32[]{:S(2)}, u32[]{:S(2)}) %collective-permute-start.29) | collective-permute-done | bytes 589856 | tf_op jit(solution)/shard_map/ppermute | solution.py:517
  199.4 2.1 fusion.21
  201.5 2.6 collective-permute-start.32
  205.4 1.7 collective-permute-start.35
  209.0 25.8 %shard_map.211 = (f32[6,208,512]{2,1,0:T(8,128)}, bf16[6,208,512]{2,1,0:T(8,128)(2,1)}, bf16[4,576,512]{2,1,0:T(8,128)(2,1)}, bf16[4,576,512]{2,1,0:T(8,128)(2,1)}, f32[8,512]{1,0:T(8,128)}, /*index=5*/f32[1,2048]{1,0:T(1,128)}) custom-call(s32[9]{0:T(128)} %pad_add_fusion.info, bf16[576,512]{1,0:T(8,128)(2,1)} %copy-done.15, bf16[576,512]{1,0:T(8,128)(2,1)} %copy-done.45, ...), custom_call_target="tpu_custom_call" | custom-call | flops 30000001024 | bytes 30000000 | tf_op jit(solution)/shard_map/pallas_call | solution.py:419
  236.1 1.6 collective-permute-start.38
  239.6 1.5 fusion.28
  241.1 1.7 collective-permute-start.41
  244.6 21.0 %shard_map.212 = (bf16[12,208,512]{2,1,0:T(8,128)(2,1)}, bf16[4,192,512]{2,1,0:T(8,128)(2,1)}, bf16[4,192,512]{2,1,0:T(8,128)(2,1)}, f32[8,512]{1,0:T(8,128)}, f32[16,64,64]{2,1,0:T(8,128)}) custom-call(s32[9]{0:T(128)} %pad_add_fusion.info, bf16[384,512]{1,0:T(8,128)(2,1)} %bitcast.7.refs_0_, bf16[384,512]{1,0:T(8,128)(2,1)} %collective-permute-done.refs_1_, ...), custom_call_target="tpu_custom_call" | custom-call | flops 30000001024 | bytes 30000000 | tf_op jit(solution)/shard_map/pallas_call | solution.py:419
  265.7 4.5 %collective-permute-done.40 = bf16[576,512]{1,0:T(8,128)(2,1)S(1)} collective-permute-done((bf16[576,512]{1,0:T(8,128)(2,1)}, bf16[576,512]{1,0:T(8,128)(2,1)S(1)}, u32[]{:S(2)}, u32[]{:S(2)}) %collective-permute-start.40) | collective-permute-done | bytes 589856 | tf_op jit(solution)/shard_map/ppermute | solution.py:517
  272.5 1.9 fusion.18
  274.4 2.7 collective-permute-start.46
  278.9 2.5 fusion.3
  281.5 2.2 fusion.42
  283.8 1.6 collective-permute-start.45
  288.0 9.7 %collective-permute-done.47 = bf16[192,512]{1,0:T(8,128)(2,1)} collective-permute-done((bf16[192,512]{1,0:T(8,128)(2,1)S(1)}, bf16[192,512]{1,0:T(8,128)(2,1)}, u32[]{:S(2)}, u32[]{:S(2)}) %collective-permute-start.47) | collective-permute-done | bytes 196640 | tf_op jit(solution)/shard_map/ppermute | solution.py:522
  297.8 1.4 collective-permute-start.49
  299.2 10.6 %collective-permute-done.46 = bf16[576,512]{1,0:T(8,128)(2,1)} collective-permute-done((bf16[576,512]{1,0:T(8,128)(2,1)S(1)}, bf16[576,512]{1,0:T(8,128)(2,1)}, u32[]{:S(2)}, u32[]{:S(2)}) %collective-permute-start.46) | collective-permute-done | bytes 589856 | tf_op jit(solution)/shard_map/ppermute | solution.py:522
  315.4 2.2 add_convert_fusion.2
  317.6 1.9 collective-permute-start.56
  319.5 3.7 %collective-permute-done.50 = bf16[192,512]{1,0:T(8,128)(2,1)S(1)} collective-permute-done((bf16[192,512]{1,0:T(8,128)(2,1)S(1)}, bf16[192,512]{1,0:T(8,128)(2,1)S(1)}, u32[]{:S(2)}, u32[]{:S(2)}) %collective-permute-start.50) | collective-permute-done | bytes 196640 | tf_op jit(solution)/shard_map/ppermute | solution.py:522
  323.8 1.7 collective-permute-start.54
  328.1 1.9 fusion.6
  329.9 2.7 reshape.332
  332.7 3.7 %copy.74 = bf16[1,4,3,14,14,512]{5,1,4,3,2,0:T(4,128)(2,1)} copy(bf16[1,4,3,14,14,512]{5,4,3,2,1,0:T(8,128)(2,1)S(1)} %reshape.332) | data formatting | bytes 4816896 | tf_op jit(solution)/shard_map/reshape | solution.py:787
  337.4 2.2 collective-permute-start.59
  356.9 1.7 broadcast_in_dim_reshape.16
  359.2 1.5 broadcast_in_dim_reshape.14
  (323 shorter events, 74.6 us)
Async XLA Ops:
  4.0 21.7 %collective-permute-start.10 = (bf16[24,128]{1,0:T(8,128)(2,1)S(1)}, bf16[24,128]{1,0:T(8,128)(2,1)S(1)}, u32[]{:S(2)}, u32[]{:S(2)}) collective-permute-start(bf16[24,128]{1,0:T(8,128)(2,1)S(1)} %fusion.55), channel_id=1, source_target_pairs={{0,8},{4,12},{8,0},{12,4},{1,9},{5,13},{9,1},{13,5},{2,10},{6,14},... | collective-permute-start | bytes 18440 | tf_op jit(solution)/shard_map/ppermute | solution.py:517
  7.0 18.7 %collective-permute-start.9 = (bf16[24,128]{1,0:T(8,128)(2,1)S(1)}, bf16[24,128]{1,0:T(8,128)(2,1)S(1)}, u32[]{:S(2)}, u32[]{:S(2)}) collective-permute-start(bf16[24,128]{1,0:T(8,128)(2,1)S(1)} %fusion.55), channel_id=1, source_target_pairs={{0,12},{4,8},{8,4},{12,0},{1,13},{5,9},{9,5},{13,1},{2,14},{6,10},... | collective-permute-start | bytes 18440 | tf_op jit(solution)/shard_map/ppermute | solution.py:517
  8.4 17.3 %collective-permute-start.8 = (bf16[24,128]{1,0:T(8,128)(2,1)S(1)}, bf16[24,128]{1,0:T(8,128)(2,1)S(1)}, u32[]{:S(2)}, u32[]{:S(2)}) collective-permute-start(bf16[24,128]{1,0:T(8,128)(2,1)S(1)} %fusion.55), channel_id=1, source_target_pairs={{0,4},{4,0},{8,12},{12,8},{1,5},{5,1},{9,13},{13,9},{2,6},{6,2},{1... | collective-permute-start | bytes 18440 | tf_op jit(solution)/shard_map/ppermute | solution.py:517
  8.5 25.7 %collective-permute-start.2 = (bf16[384,512]{1,0:T(8,128)(2,1)}, bf16[384,512]{1,0:T(8,128)(2,1)}, u32[]{:S(2)}, u32[]{:S(2)}) collective-permute-start(bf16[384,512]{1,0:T(8,128)(2,1)} %bitcast.7.refs_0_), channel_id=1, source_target_pairs={{0,12},{4,8},{8,4},{12,0},{1,13},{5,9},{9,5},{13,1},{2,14},{6,10},... | collective-permute-start | bytes 1179656 | tf_op jit(solution)/shard_map/ppermute | solution.py:517
  11.4 23.0 %collective-permute-start.1 = (bf16[384,512]{1,0:T(8,128)(2,1)}, bf16[384,512]{1,0:T(8,128)(2,1)}, u32[]{:S(2)}, u32[]{:S(2)}) collective-permute-start(bf16[384,512]{1,0:T(8,128)(2,1)} %bitcast.7.refs_0_), channel_id=1, source_target_pairs={{0,8},{4,12},{8,0},{12,4},{1,9},{5,13},{9,1},{13,5},{2,10},{6,14},... | collective-permute-start | bytes 1179656 | tf_op jit(solution)/shard_map/ppermute | solution.py:517
  25.6 9.8 %collective-permute-start = (bf16[384,512]{1,0:T(8,128)(2,1)}, bf16[384,512]{1,0:T(8,128)(2,1)}, u32[]{:S(2)}, u32[]{:S(2)}) collective-permute-start(bf16[384,512]{1,0:T(8,128)(2,1)} %bitcast.7.refs_0_), channel_id=1, source_target_pairs={{0,4},{4,0},{8,12},{12,8},{1,5},{5,1},{9,13},{13,9},{2,6},{6,2},{1... | collective-permute-start | bytes 1179656 | tf_op jit(solution)/shard_map/ppermute | solution.py:517
  25.7 15.6 %collective-permute-start.7 = (bf16[12,208,512]{2,1,0:T(8,128)(2,1)}, bf16[12,208,512]{2,1,0:T(8,128)(2,1)}, u32[]{:S(2)}, u32[]{:S(2)}) collective-permute-start(bf16[12,208,512]{2,1,0:T(8,128)(2,1)} %pad.21.refs_8_), channel_id=1, source_target_pairs={{0,16},{16,0},{1,17},{17,1},{2,18},{18,2},{3,19},{19,3},{4,20},{20... | collective-permute-start | bytes 7667720 | tf_op jit(solution)/shard_map/ppermute | solution.py:513
  34.4 5.7 %collective-permute-start.6 = (bf16[384,512]{1,0:T(8,128)(2,1)}, bf16[384,512]{1,0:T(8,128)(2,1)S(1)}, u32[]{:S(2)}, u32[]{:S(2)}) collective-permute-start(bf16[384,512]{1,0:T(8,128)(2,1)} %collective-permute-done.2.refs_3_), channel_id=1, source_target_pairs={{0,16},{16,0},{1,17},{17,1},{2,18},{18,2},{3,19},{19,3},{4,20},{20... | collective-permute-start | bytes 1179656 | tf_op jit(solution)/shard_map/ppermute | solution.py:513
  35.4 5.9 %collective-permute-start.4 = (bf16[384,512]{1,0:T(8,128)(2,1)}, bf16[384,512]{1,0:T(8,128)(2,1)S(1)}, u32[]{:S(2)}, u32[]{:S(2)}) collective-permute-start(bf16[384,512]{1,0:T(8,128)(2,1)} %collective-permute-done.refs_1_), channel_id=1, source_target_pairs={{0,16},{16,0},{1,17},{17,1},{2,18},{18,2},{3,19},{19,3},{4,20},{20... | collective-permute-start | bytes 1179656 | tf_op jit(solution)/shard_map/ppermute | solution.py:513
  37.7 18.9 %collective-permute-start.15 = (bf16[576,512]{1,0:T(8,128)(2,1)S(1)}, bf16[576,512]{1,0:T(8,128)(2,1)S(1)}, u32[]{:S(2)}, u32[]{:S(2)}) collective-permute-start(bf16[576,512]{1,0:T(8,128)(2,1)S(1)} %get-tuple-element.127.refs_0_), channel_id=1, source_target_pairs={{0,12},{4,8},{8,4},{12,0},{1,13},{5,9},{9,5},{13,1},{2,14},{6,10},... | collective-permute-start | bytes 1769480 | tf_op jit(solution)/shard_map/ppermute | solution.py:517
  40.1 26.5 %collective-permute-start.14 = (bf16[576,512]{1,0:T(8,128)(2,1)S(1)}, bf16[576,512]{1,0:T(8,128)(2,1)S(1)}, u32[]{:S(2)}, u32[]{:S(2)}) collective-permute-start(bf16[576,512]{1,0:T(8,128)(2,1)S(1)} %get-tuple-element.127.refs_0_), channel_id=1, source_target_pairs={{0,8},{4,12},{8,0},{12,4},{1,9},{5,13},{9,1},{13,5},{2,10},{6,14},... | collective-permute-start | bytes 1769480 | tf_op jit(solution)/shard_map/ppermute | solution.py:517
  40.6 26.1 %collective-permute-start.13 = (bf16[576,512]{1,0:T(8,128)(2,1)S(1)}, bf16[576,512]{1,0:T(8,128)(2,1)S(1)}, u32[]{:S(2)}, u32[]{:S(2)}) collective-permute-start(bf16[576,512]{1,0:T(8,128)(2,1)S(1)} %get-tuple-element.127.refs_0_), channel_id=1, source_target_pairs={{0,4},{4,0},{8,12},{12,8},{1,5},{5,1},{9,13},{13,9},{2,6},{6,2},{1... | collective-permute-start | bytes 1769480 | tf_op jit(solution)/shard_map/ppermute | solution.py:517
  68.9 23.7 %collective-permute-start.22 = (bf16[576,512]{1,0:T(8,128)(2,1)S(1)}, bf16[576,512]{1,0:T(8,128)(2,1)S(1)}, u32[]{:S(2)}, u32[]{:S(2)}) collective-permute-start(bf16[576,512]{1,0:T(8,128)(2,1)S(1)} %get-tuple-element.135.refs_0_), channel_id=1, source_target_pairs={{0,12},{4,8},{8,4},{12,0},{1,13},{5,9},{9,5},{13,1},{2,14},{6,10},... | collective-permute-start | bytes 1769480 | tf_op jit(solution)/shard_map/ppermute | solution.py:517
  70.6 27.1 %collective-permute-start.21 = (bf16[576,512]{1,0:T(8,128)(2,1)S(1)}, bf16[576,512]{1,0:T(8,128)(2,1)S(1)}, u32[]{:S(2)}, u32[]{:S(2)}) collective-permute-start(bf16[576,512]{1,0:T(8,128)(2,1)S(1)} %get-tuple-element.135.refs_0_), channel_id=1, source_target_pairs={{0,8},{4,12},{8,0},{12,4},{1,9},{5,13},{9,1},{13,5},{2,10},{6,14},... | collective-permute-start | bytes 1769480 | tf_op jit(solution)/shard_map/ppermute | solution.py:517
  71.8 26.0 %collective-permute-start.20 = (bf16[576,512]{1,0:T(8,128)(2,1)S(1)}, bf16[576,512]{1,0:T(8,128)(2,1)S(1)}, u32[]{:S(2)}, u32[]{:S(2)}) collective-permute-start(bf16[576,512]{1,0:T(8,128)(2,1)S(1)} %get-tuple-element.135.refs_0_), channel_id=1, source_target_pairs={{0,4},{4,0},{8,12},{12,8},{1,5},{5,1},{9,13},{13,9},{2,6},{6,2},{1... | collective-permute-start | bytes 1769480 | tf_op jit(solution)/shard_map/ppermute | solution.py:517
  97.8 15.4 %collective-permute-start.23 = (bf16[576,512]{1,0:T(8,128)(2,1)S(1)}, bf16[576,512]{1,0:T(8,128)(2,1)S(1)}, u32[]{:S(2)}, u32[]{:S(2)}) collective-permute-start(bf16[576,512]{1,0:T(8,128)(2,1)S(1)} %get-tuple-element.135.refs_0_), channel_id=1, source_target_pairs={{0,16},{16,0},{1,17},{17,1},{2,18},{18,2},{3,19},{19,3},{4,20},{20... | collective-permute-start | bytes 1769480 | tf_op jit(solution)/shard_map/ppermute | solution.py:513
  97.9 15.4 %collective-permute-start.24 = (bf16[576,512]{1,0:T(8,128)(2,1)S(1)}, bf16[576,512]{1,0:T(8,128)(2,1)S(1)}, u32[]{:S(2)}, u32[]{:S(2)}) collective-permute-start(bf16[576,512]{1,0:T(8,128)(2,1)S(1)} %collective-permute-done.20.refs_1_), channel_id=1, source_target_pairs={{0,16},{16,0},{1,17},{17,1},{2,18},{18,2},{3,19},{19,3},{4,20},{20... | collective-permute-start | bytes 1769480 | tf_op jit(solution)/shard_map/ppermute | solution.py:513
  98.4 15.0 %collective-permute-start.25 = (bf16[576,512]{1,0:T(8,128)(2,1)S(1)}, bf16[576,512]{1,0:T(8,128)(2,1)S(1)}, u32[]{:S(2)}, u32[]{:S(2)}) collective-permute-start(bf16[576,512]{1,0:T(8,128)(2,1)S(1)} %collective-permute-done.21.refs_2_), channel_id=1, source_target_pairs={{0,16},{16,0},{1,17},{17,1},{2,18},{18,2},{3,19},{19,3},{4,20},{20... | collective-permute-start | bytes 1769480 | tf_op jit(solution)/shard_map/ppermute | solution.py:513
  98.4 14.9 %collective-permute-start.26 = (bf16[576,512]{1,0:T(8,128)(2,1)S(1)}, bf16[576,512]{1,0:T(8,128)(2,1)S(1)}, u32[]{:S(2)}, u32[]{:S(2)}) collective-permute-start(bf16[576,512]{1,0:T(8,128)(2,1)S(1)} %collective-permute-done.22.refs_3_), channel_id=1, source_target_pairs={{0,16},{16,0},{1,17},{17,1},{2,18},{18,2},{3,19},{19,3},{4,20},{20... | collective-permute-start | bytes 1769480 | tf_op jit(solution)/shard_map/ppermute | solution.py:513
  166.8 24.6 %collective-permute-start.30 = (bf16[576,512]{1,0:T(8,128)(2,1)S(1)}, bf16[576,512]{1,0:T(8,128)(2,1)}, u32[]{:S(2)}, u32[]{:S(2)}) collective-permute-start(bf16[576,512]{1,0:T(8,128)(2,1)S(1)} %get-tuple-element.234), channel_id=1, source_target_pairs={{0,12},{4,8},{8,4},{12,0},{1,13},{5,9},{9,5},{13,1},{2,14},{6,10},... | collective-permute-start | bytes 1769480 | tf_op jit(solution)/shard_map/ppermute | solution.py:517
  168.5 27.3 %collective-permute-start.29 = (bf16[576,512]{1,0:T(8,128)(2,1)S(1)}, bf16[576,512]{1,0:T(8,128)(2,1)}, u32[]{:S(2)}, u32[]{:S(2)}) collective-permute-start(bf16[576,512]{1,0:T(8,128)(2,1)S(1)} %get-tuple-element.235), channel_id=1, source_target_pairs={{0,8},{4,12},{8,0},{12,4},{1,9},{5,13},{9,1},{13,5},{2,10},{6,14},... | collective-permute-start | bytes 1769480 | tf_op jit(solution)/shard_map/ppermute | solution.py:517
  169.7 26.2 %collective-permute-start.28 = (bf16[576,512]{1,0:T(8,128)(2,1)S(1)}, bf16[576,512]{1,0:T(8,128)(2,1)}, u32[]{:S(2)}, u32[]{:S(2)}) collective-permute-start(bf16[576,512]{1,0:T(8,128)(2,1)S(1)} %get-tuple-element.236), channel_id=1, source_target_pairs={{0,4},{4,0},{8,12},{12,8},{1,5},{5,1},{9,13},{13,9},{2,6},{6,2},{1... | collective-permute-start | bytes 1769480 | tf_op jit(solution)/shard_map/ppermute | solution.py:517
  195.9 8.2 %collective-permute-start.31 = (bf16[4,192,512]{2,1,0:T(8,128)(2,1)}, bf16[4,192,512]{2,1,0:T(8,128)(2,1)}, u32[]{:S(2)}, u32[]{:S(2)}) collective-permute-start(bf16[4,192,512]{2,1,0:T(8,128)(2,1)} %get-tuple-element.157), channel_id=1, source_target_pairs={{0,16},{16,0},{1,17},{17,1},{2,18},{18,2},{3,19},{19,3},{4,20},{20... | collective-permute-start | bytes 2359304 | tf_op jit(solution)/shard_map/ppermute | solution.py:513
  201.5 33.3 %collective-permute-start.32 = (bf16[576,512]{1,0:T(8,128)(2,1)S(1)}, bf16[576,512]{1,0:T(8,128)(2,1)S(1)}, u32[]{:S(2)}, u32[]{:S(2)}) collective-permute-start(bf16[576,512]{1,0:T(8,128)(2,1)S(1)} %fusion.21), channel_id=1, source_target_pairs={{0,2},{1,3},{2,0},{3,1},{4,6},{5,7},{6,4},{7,5},{8,10},{9,11},{10,... | collective-permute-start | bytes 1769480 | tf_op jit(solution)/shard_map/ppermute | solution.py:522
  205.4 29.3 %collective-permute-start.35 = (bf16[192,512]{1,0:T(8,128)(2,1)S(1)}, bf16[192,512]{1,0:T(8,128)(2,1)S(1)}, u32[]{:S(2)}, u32[]{:S(2)}) collective-permute-start(bf16[192,512]{1,0:T(8,128)(2,1)S(1)} %get-tuple-element.246), channel_id=1, source_target_pairs={{0,12},{4,8},{8,4},{12,0},{1,13},{5,9},{9,5},{13,1},{2,14},{6,10},... | collective-permute-start | bytes 589832 | tf_op jit(solution)/shard_map/ppermute | solution.py:517
  207.1 27.6 %collective-permute-start.34 = (bf16[192,512]{1,0:T(8,128)(2,1)S(1)}, bf16[192,512]{1,0:T(8,128)(2,1)S(1)}, u32[]{:S(2)}, u32[]{:S(2)}) collective-permute-start(bf16[192,512]{1,0:T(8,128)(2,1)S(1)} %get-tuple-element.247), channel_id=1, source_target_pairs={{0,8},{4,12},{8,0},{12,4},{1,9},{5,13},{9,1},{13,5},{2,10},{6,14},... | collective-permute-start | bytes 589832 | tf_op jit(solution)/shard_map/ppermute | solution.py:517
  208.3 26.5 %collective-permute-start.33 = (bf16[192,512]{1,0:T(8,128)(2,1)S(1)}, bf16[192,512]{1,0:T(8,128)(2,1)S(1)}, u32[]{:S(2)}, u32[]{:S(2)}) collective-permute-start(bf16[192,512]{1,0:T(8,128)(2,1)S(1)} %get-tuple-element.248), channel_id=1, source_target_pairs={{0,4},{4,0},{8,12},{12,8},{1,5},{5,1},{9,13},{13,9},{2,6},{6,2},{1... | collective-permute-start | bytes 589832 | tf_op jit(solution)/shard_map/ppermute | solution.py:517
  236.1 29.5 %collective-permute-start.38 = (bf16[192,512]{1,0:T(8,128)(2,1)S(1)}, bf16[192,512]{1,0:T(8,128)(2,1)S(1)}, u32[]{:S(2)}, u32[]{:S(2)}) collective-permute-start(bf16[192,512]{1,0:T(8,128)(2,1)S(1)} %fusion.35), channel_id=1, source_target_pairs={{0,1},{1,0},{2,3},{3,2},{4,5},{5,4},{6,7},{7,6},{8,9},{9,8},{10,11... | collective-permute-start | bytes 589832 | tf_op jit(solution)/shard_map/ppermute | solution.py:522
  237.9 27.8 %collective-permute-start.37 = (bf16[576,512]{1,0:T(8,128)(2,1)S(1)}, bf16[576,512]{1,0:T(8,128)(2,1)S(1)}, u32[]{:S(2)}, u32[]{:S(2)}) collective-permute-start(bf16[576,512]{1,0:T(8,128)(2,1)S(1)} %add_convert_fusion.7), channel_id=1, source_target_pairs={{0,1},{1,0},{2,3},{3,2},{4,5},{5,4},{6,7},{7,6},{8,9},{9,8},{10,11... | collective-permute-start | bytes 1769480 | tf_op jit(solution)/shard_map/ppermute | solution.py:522
  241.1 24.6 %collective-permute-start.41 = (bf16[576,512]{1,0:T(8,128)(2,1)}, bf16[576,512]{1,0:T(8,128)(2,1)S(1)}, u32[]{:S(2)}, u32[]{:S(2)}) collective-permute-start(bf16[576,512]{1,0:T(8,128)(2,1)} %get-tuple-element.231), channel_id=1, source_target_pairs={{0,12},{4,8},{8,4},{12,0},{1,13},{5,9},{9,5},{13,1},{2,14},{6,10},... | collective-permute-start | bytes 1769480 | tf_op jit(solution)/shard_map/ppermute | solution.py:517
  242.7 27.5 %collective-permute-start.40 = (bf16[576,512]{1,0:T(8,128)(2,1)}, bf16[576,512]{1,0:T(8,128)(2,1)S(1)}, u32[]{:S(2)}, u32[]{:S(2)}) collective-permute-start(bf16[576,512]{1,0:T(8,128)(2,1)} %get-tuple-element.232), channel_id=1, source_target_pairs={{0,8},{4,12},{8,0},{12,4},{1,9},{5,13},{9,1},{13,5},{2,10},{6,14},... | collective-permute-start | bytes 1769480 | tf_op jit(solution)/shard_map/ppermute | solution.py:517
  243.9 26.3 %collective-permute-start.39 = (bf16[576,512]{1,0:T(8,128)(2,1)}, bf16[576,512]{1,0:T(8,128)(2,1)S(1)}, u32[]{:S(2)}, u32[]{:S(2)}) collective-permute-start(bf16[576,512]{1,0:T(8,128)(2,1)} %get-tuple-element.233), channel_id=1, source_target_pairs={{0,4},{4,0},{8,12},{12,8},{1,5},{5,1},{9,13},{13,9},{2,6},{6,2},{1... | collective-permute-start | bytes 1769480 | tf_op jit(solution)/shard_map/ppermute | solution.py:517
  270.2 6.8 %collective-permute-start.42 = (bf16[4,192,512]{2,1,0:T(8,128)(2,1)}, bf16[4,192,512]{2,1,0:T(8,128)(2,1)S(1)}, u32[]{:S(2)}, u32[]{:S(2)}) collective-permute-start(bf16[4,192,512]{2,1,0:T(8,128)(2,1)} %get-tuple-element.196), channel_id=1, source_target_pairs={{0,16},{16,0},{1,17},{17,1},{2,18},{18,2},{3,19},{19,3},{4,20},{20... | collective-permute-start | bytes 2359304 | tf_op jit(solution)/shard_map/ppermute | solution.py:513
  272.1 25.7 %collective-permute-start.47 = (bf16[192,512]{1,0:T(8,128)(2,1)S(1)}, bf16[192,512]{1,0:T(8,128)(2,1)}, u32[]{:S(2)}, u32[]{:S(2)}) collective-permute-start(bf16[192,512]{1,0:T(8,128)(2,1)S(1)} %add_convert_fusion.16), channel_id=1, source_target_pairs={{0,2},{1,3},{2,0},{3,1},{4,6},{5,7},{6,4},{7,5},{8,10},{9,11},{10,... | collective-permute-start | bytes 589832 | tf_op jit(solution)/shard_map/ppermute | solution.py:522
  274.4 35.4 %collective-permute-start.46 = (bf16[576,512]{1,0:T(8,128)(2,1)S(1)}, bf16[576,512]{1,0:T(8,128)(2,1)}, u32[]{:S(2)}, u32[]{:S(2)}) collective-permute-start(bf16[576,512]{1,0:T(8,128)(2,1)S(1)} %fusion.18), channel_id=1, source_target_pairs={{0,2},{1,3},{2,0},{3,1},{4,6},{5,7},{6,4},{7,5},{8,10},{9,11},{10,... | collective-permute-start | bytes 1769480 | tf_op jit(solution)/shard_map/ppermute | solution.py:522
  283.8 26.1 %collective-permute-start.45 = (bf16[192,512]{1,0:T(8,128)(2,1)}, bf16[192,512]{1,0:T(8,128)(2,1)}, u32[]{:S(2)}, u32[]{:S(2)}) collective-permute-start(bf16[192,512]{1,0:T(8,128)(2,1)} %get-tuple-element.243), channel_id=1, source_target_pairs={{0,12},{4,8},{8,4},{12,0},{1,13},{5,9},{9,5},{13,1},{2,14},{6,10},... | collective-permute-start | bytes 589832 | tf_op jit(solution)/shard_map/ppermute | solution.py:517
  285.4 24.4 %collective-permute-start.44 = (bf16[192,512]{1,0:T(8,128)(2,1)}, bf16[192,512]{1,0:T(8,128)(2,1)}, u32[]{:S(2)}, u32[]{:S(2)}) collective-permute-start(bf16[192,512]{1,0:T(8,128)(2,1)} %get-tuple-element.244), channel_id=1, source_target_pairs={{0,8},{4,12},{8,0},{12,4},{1,9},{5,13},{9,1},{13,5},{2,10},{6,14},... | collective-permute-start | bytes 589832 | tf_op jit(solution)/shard_map/ppermute | solution.py:517
  286.6 23.3 %collective-permute-start.43 = (bf16[192,512]{1,0:T(8,128)(2,1)}, bf16[192,512]{1,0:T(8,128)(2,1)}, u32[]{:S(2)}, u32[]{:S(2)}) collective-permute-start(bf16[192,512]{1,0:T(8,128)(2,1)} %get-tuple-element.245), channel_id=1, source_target_pairs={{0,4},{4,0},{8,12},{12,8},{1,5},{5,1},{9,13},{13,9},{2,6},{6,2},{1... | collective-permute-start | bytes 589832 | tf_op jit(solution)/shard_map/ppermute | solution.py:517
  297.8 29.6 %collective-permute-start.49 = (bf16[12,208,512]{2,1,0:T(8,128)(2,1)S(1)}, bf16[12,208,512]{2,1,0:T(8,128)(2,1)S(1)}, u32[]{:S(2)}, u32[]{:S(2)}) collective-permute-start(bf16[12,208,512]{2,1,0:T(8,128)(2,1)S(1)} %copy-done.3), channel_id=1, source_target_pairs={{0,16},{1,17},{2,18},{3,19},{4,20},{5,21},{6,22},{7,23},{8,24},{9,... | collective-permute-start | bytes 7667720 | tf_op jit(solution)/shard_map/ppermute | solution.py:724
  309.8 18.2 %collective-permute-start.48 = (bf16[12,208,512]{2,1,0:T(8,128)(2,1)}, bf16[12,208,512]{2,1,0:T(8,128)(2,1)S(1)}, u32[]{:S(2)}, u32[]{:S(2)}) collective-permute-start(bf16[12,208,512]{2,1,0:T(8,128)(2,1)} %get-tuple-element.209), channel_id=1, source_target_pairs={{16,0},{17,1},{18,2},{19,3},{20,4},{21,5},{22,6},{23,7},{24,8},{25... | collective-permute-start | bytes 7667720 | tf_op jit(solution)/shard_map/ppermute | solution.py:780
  312.6 6.9 %collective-permute-start.51 = (f32[144,128]{1,0:T(8,128)S(1)}, f32[144,128]{1,0:T(8,128)S(1)}, u32[]{:S(2)}, u32[]{:S(2)}) collective-permute-start(f32[144,128]{1,0:T(8,128)S(1)} %copy-done.20), channel_id=1, source_target_pairs={{0,16},{16,0},{1,17},{17,1},{2,18},{18,2},{3,19},{19,3},{4,20},{20... | collective-permute-start | bytes 221192 | tf_op jit(solution)/shard_map/ppermute | solution.py:513
  315.3 7.8 %collective-permute-start.50 = (bf16[192,512]{1,0:T(8,128)(2,1)S(1)}, bf16[192,512]{1,0:T(8,128)(2,1)S(1)}, u32[]{:S(2)}, u32[]{:S(2)}) collective-permute-start(bf16[192,512]{1,0:T(8,128)(2,1)S(1)} %fusion.32), channel_id=1, source_target_pairs={{0,1},{1,0},{2,3},{3,2},{4,5},{5,4},{6,7},{7,6},{8,9},{9,8},{10,11... | collective-permute-start | bytes 589832 | tf_op jit(solution)/shard_map/ppermute | solution.py:522
  317.6 25.3 %collective-permute-start.56 = (bf16[576,512]{1,0:T(8,128)(2,1)}, bf16[576,512]{1,0:T(8,128)(2,1)}, u32[]{:S(2)}, u32[]{:S(2)}) collective-permute-start(bf16[576,512]{1,0:T(8,128)(2,1)} %add_convert_fusion.2), channel_id=1, source_target_pairs={{0,1},{1,0},{2,3},{3,2},{4,5},{5,4},{6,7},{7,6},{8,9},{9,8},{10,11... | collective-permute-start | bytes 1769480 | tf_op jit(solution)/shard_map/ppermute | solution.py:522
  323.8 12.6 %collective-permute-start.54 = (f32[144,128]{1,0:T(8,128)}, f32[144,128]{1,0:T(8,128)}, u32[]{:S(2)}, u32[]{:S(2)}) collective-permute-start(f32[144,128]{1,0:T(8,128)} %add.223), channel_id=1, source_target_pairs={{0,12},{4,8},{8,4},{12,0},{1,13},{5,9},{9,5},{13,1},{2,14},{6,10},... | collective-permute-start | bytes 221192 | tf_op jit(solution)/shard_map/ppermute | solution.py:517
  325.5 10.9 %collective-permute-start.53 = (f32[144,128]{1,0:T(8,128)}, f32[144,128]{1,0:T(8,128)}, u32[]{:S(2)}, u32[]{:S(2)}) collective-permute-start(f32[144,128]{1,0:T(8,128)} %add.223), channel_id=1, source_target_pairs={{0,8},{4,12},{8,0},{12,4},{1,9},{5,13},{9,1},{13,5},{2,10},{6,14},... | collective-permute-start | bytes 221192 | tf_op jit(solution)/shard_map/ppermute | solution.py:517
  327.4 9.0 %collective-permute-start.52 = (f32[144,128]{1,0:T(8,128)}, f32[144,128]{1,0:T(8,128)}, u32[]{:S(2)}, u32[]{:S(2)}) collective-permute-start(f32[144,128]{1,0:T(8,128)} %add.223), channel_id=1, source_target_pairs={{0,4},{4,0},{8,12},{12,8},{1,5},{5,1},{9,13},{13,9},{2,6},{6,2},{1... | collective-permute-start | bytes 221192 | tf_op jit(solution)/shard_map/ppermute | solution.py:517
  328.0 14.8 %collective-permute-start.55 = (bf16[192,512]{1,0:T(8,128)(2,1)}, bf16[192,512]{1,0:T(8,128)(2,1)}, u32[]{:S(2)}, u32[]{:S(2)}) collective-permute-start(bf16[192,512]{1,0:T(8,128)(2,1)} %add_convert_fusion.14), channel_id=1, source_target_pairs={{0,2},{1,3},{2,0},{3,1},{4,6},{5,7},{6,4},{7,5},{8,10},{9,11},{10,... | collective-permute-start | bytes 589832 | tf_op jit(solution)/shard_map/ppermute | solution.py:522
  337.4 6.3 %collective-permute-start.59 = (f32[144,128]{1,0:T(8,128)S(1)}, f32[144,128]{1,0:T(8,128)S(1)}, u32[]{:S(2)}, u32[]{:S(2)}) collective-permute-start(f32[144,128]{1,0:T(8,128)S(1)} %add_add_fusion.1), channel_id=1, source_target_pairs={{0,3},{1,2},{2,1},{3,0},{4,7},{5,6},{6,5},{7,4},{8,11},{9,10},{10,... | collective-permute-start | bytes 221192 | tf_op jit(solution)/shard_map/ppermute | solution.py:522
  (75 other events, 557.8 us)
